TPU v7x, 32 devices: a whole 2x2x4 slice. The times are simulated.
32 devices in a mesh: ctx: 16 (over z, y, core), tp: 2 (over x).
Axes of the slice: x: 2, y: 2, z: 4, core: 2. Of those that a mesh axis runs over, the one named last changes fastest.
Arguments:
- query_in: bfloat16 [4096, 8192], P('ctx', 'tp'), may hold values from -6 to 6
- key_in: bfloat16 [4096, 8192], P('ctx', 'tp'), may hold values from -6 to 6
- value_in: bfloat16 [4096, 8192], P('ctx', 'tp'), may hold values from -6 to 6
- cotangent: bfloat16 [4096, 8192], P('ctx', 'tp'), may hold values from -6 to 6
- short_weight: float32 [3, 3, 8192], P(None, None, 'tp'), may hold values from -3 to 3
- long_filter: bfloat16 [4096, 8192], P('ctx', 'tp'), may hold values from -1.5 to 1.5
Outputs:
- block_out: bfloat16 [4096, 8192], P('ctx', 'tp')
- grad_query: bfloat16 [4096, 8192], P('ctx', 'tp')
- grad_key: bfloat16 [4096, 8192], P('ctx', 'tp')
- grad_value: bfloat16 [4096, 8192], P('ctx', 'tp')
- grad_short: float32 [3, 3, 8192], P(None, None, 'tp')
- grad_filter: bfloat16 [4096, 8192], P('ctx', 'tp')
All inputs are finite; a program needn't handle non-finite values.
Results may differ from a plain program's by a relative error of at most 0.025.
Values may be sent and summed in bfloat16 or wider, within the bound.
A program may use at most 192 MiB of HBM per device.

v0:
```python
import math

import jax
import jax.numpy as jnp
from jax import lax
from jax.sharding import PartitionSpec as P

S = 128


def from_behind(x, axis, by):
    count = lax.axis_size(axis)
    pairs = [(i, i + by) for i in range(count) if 0 <= i + by < count]
    return lax.ppermute(x, axis, pairs)


def phase_grid(left_index, right_index, period):
    product = left_index[:, None] * right_index[None, :] % period
    phases = 2.0 * math.pi / period * product.astype(jnp.float32)
    return (jnp.cos(phases), jnp.sin(phases))


def short_filter(extended, weights, local_rows):
    tap_count = weights.shape[0]
    result = jnp.zeros((local_rows, extended.shape[1]), jnp.float32)
    for lag_index in range(tap_count):
        offset_row = tap_count - 1 - lag_index
        result = result + weights[lag_index] * extended[
            offset_row : offset_row + local_rows
        ].astype(jnp.float32)
    return result


def filter_back(extended, weights, local_rows):
    tap_count = weights.shape[0]
    result = jnp.zeros((local_rows, extended.shape[1]), jnp.float32)
    for lag_index in range(tap_count):
        result = result + weights[lag_index] * extended[lag_index : lag_index + local_rows].astype(
            jnp.float32
        )
    return result


def weight_terms(grads, extended, tap_count, local_rows):
    grad_float = grads.astype(jnp.float32)
    terms = []
    for lag_index in range(tap_count):
        offset_row = tap_count - 1 - lag_index
        terms.append(
            jnp.sum(
                grad_float * extended[offset_row : offset_row + local_rows].astype(jnp.float32),
                axis=0,
            )
        )
    return jnp.stack(terms)


def spectral_product(spec_re, spec_im, filt_re, filt_im):
    spec_re = spec_re.astype(jnp.float32)
    spec_im = spec_im.astype(jnp.float32)
    prod_re = spec_re * filt_re - spec_im * filt_im
    prod_im = spec_re * filt_im + spec_im * filt_re
    return (prod_re.astype(jnp.bfloat16), prod_im.astype(jnp.bfloat16))


def on_device(query_in, key_in, value_in, cotangent, short_weight, long_filter):
    local_rows, channels = query_in.shape
    tap_count = short_weight.shape[1]
    rim_rows = tap_count - 1
    ctx_size = lax.axis_size("ctx")
    ctx_rank = lax.axis_index("ctx")
    length = local_rows * ctx_size
    fft_size = 2 * length
    inner_len = S
    outer_len = fft_size // inner_len
    half_rows = outer_len // 2
    inv_root = 1.0 / math.sqrt(length)
    outer_ids = jnp.arange(outer_len, dtype=jnp.int32)
    half_ids = jnp.arange(half_rows, dtype=jnp.int32)
    inner_ids = jnp.arange(inner_len, dtype=jnp.int32)
    cos_first, sin_first = phase_grid(outer_ids, half_ids, outer_len)
    cos_first = cos_first.astype(jnp.bfloat16)
    sin_first = sin_first.astype(jnp.bfloat16)
    cos_back, sin_back = phase_grid(half_ids, outer_ids, outer_len)
    cos_back = cos_back.astype(jnp.bfloat16)
    sin_back = sin_back.astype(jnp.bfloat16)
    cos_inner, sin_inner = phase_grid(inner_ids, inner_ids, inner_len)
    cos_inner = cos_inner.astype(jnp.bfloat16)
    sin_inner = sin_inner.astype(jnp.bfloat16)
    ahead = from_behind(
        (
            query_in[local_rows - rim_rows :],
            key_in[local_rows - rim_rows :],
            value_in[local_rows - rim_rows :],
        ),
        "ctx",
        1,
    )
    ext_query = jnp.concatenate([ahead[0], query_in], axis=0)
    ext_key = jnp.concatenate([ahead[1], key_in], axis=0)
    ext_value = jnp.concatenate([ahead[2], value_in], axis=0)
    q_short = short_filter(ext_query, short_weight[0], local_rows)
    k_short = short_filter(ext_key, short_weight[1], local_rows)
    v_short = short_filter(ext_value, short_weight[2], local_rows)
    mixed = (k_short * v_short).astype(jnp.bfloat16)
    inner_part = inner_len // ctx_size
    k_rows = outer_len // ctx_size
    row_ids = ctx_rank * k_rows + jnp.arange(k_rows, dtype=jnp.int32)
    fwd_cos, fwd_sin = phase_grid(
        outer_ids, ctx_rank * inner_part + jnp.arange(inner_part, dtype=jnp.int32), fft_size
    )
    fwd_cos = fwd_cos[:, :, None]
    fwd_sin = fwd_sin[:, :, None]
    inv_cos, inv_sin = phase_grid(row_ids, inner_ids, fft_size)
    inv_cos = inv_cos[:, :, None]
    inv_sin = inv_sin[:, :, None]

    def forward_transform(signal):
        grid_rows = signal.reshape(local_rows // inner_len, inner_len, channels)
        arrived = lax.all_to_all(grid_rows, "ctx", split_axis=1, concat_axis=0, tiled=True)
        flattened = arrived.reshape(half_rows, inner_part * channels)
        first_re = jnp.dot(cos_first, flattened, preferred_element_type=jnp.float32).reshape(
            outer_len, inner_part, channels
        )
        first_im = -jnp.dot(sin_first, flattened, preferred_element_type=jnp.float32).reshape(
            outer_len, inner_part, channels
        )
        twist_re = (first_re * fwd_cos + first_im * fwd_sin).astype(jnp.bfloat16)
        twist_im = (first_im * fwd_cos - first_re * fwd_sin).astype(jnp.bfloat16)
        spread = (
            lax.all_to_all(twist_re, "ctx", split_axis=0, concat_axis=1, tiled=True),
            lax.all_to_all(twist_im, "ctx", split_axis=0, concat_axis=1, tiled=True),
        )
        spec_re = jnp.einsum(
            "js,ksc->kjc", cos_inner, spread[0], preferred_element_type=jnp.float32
        ) + jnp.einsum("js,ksc->kjc", sin_inner, spread[1], preferred_element_type=jnp.float32)
        spec_im = jnp.einsum(
            "js,ksc->kjc", cos_inner, spread[1], preferred_element_type=jnp.float32
        ) - jnp.einsum("js,ksc->kjc", sin_inner, spread[0], preferred_element_type=jnp.float32)
        return (spec_re.astype(jnp.bfloat16), spec_im.astype(jnp.bfloat16))

    def inverse_transform(spec_re, spec_im):
        back_re = jnp.einsum(
            "sj,kjc->ksc", cos_inner, spec_re, preferred_element_type=jnp.float32
        ) - jnp.einsum("sj,kjc->ksc", sin_inner, spec_im, preferred_element_type=jnp.float32)
        back_im = jnp.einsum(
            "sj,kjc->ksc", cos_inner, spec_im, preferred_element_type=jnp.float32
        ) + jnp.einsum("sj,kjc->ksc", sin_inner, spec_re, preferred_element_type=jnp.float32)
        untw_re = (back_re * inv_cos - back_im * inv_sin).astype(jnp.bfloat16)
        untw_im = (back_im * inv_cos + back_re * inv_sin).astype(jnp.bfloat16)
        arrived = (
            lax.all_to_all(untw_re, "ctx", split_axis=1, concat_axis=0, tiled=True),
            lax.all_to_all(untw_im, "ctx", split_axis=1, concat_axis=0, tiled=True),
        )
        signal = jnp.dot(
            cos_back,
            arrived[0].reshape(outer_len, inner_part * channels),
            preferred_element_type=jnp.float32,
        ) - jnp.dot(
            sin_back,
            arrived[1].reshape(outer_len, inner_part * channels),
            preferred_element_type=jnp.float32,
        )
        signal = (
            (signal * (1.0 / fft_size))
            .astype(jnp.bfloat16)
            .reshape(half_rows, inner_part, channels)
        )
        returned = lax.all_to_all(signal, "ctx", split_axis=0, concat_axis=1, tiled=True)
        return returned.reshape(local_rows, channels)

    spec_h = forward_transform(long_filter)
    h_re = spec_h[0].astype(jnp.float32)
    h_im = spec_h[1].astype(jnp.float32)
    spec_x = forward_transform(mixed)
    product = spectral_product(spec_x[0], spec_x[1], h_re, h_im)
    conv = inverse_transform(product[0], product[1]).astype(jnp.float32)
    block_out = (q_short * conv).astype(jnp.bfloat16)
    cot_float = cotangent.astype(jnp.float32)
    gq_short = (cot_float * conv).astype(jnp.bfloat16)
    grad_conv = (cot_float * q_short).astype(jnp.bfloat16)
    spec_g = forward_transform(grad_conv)
    back_product = spectral_product(spec_g[0], spec_g[1], h_re, -h_im)
    grad_mixed = inverse_transform(back_product[0], back_product[1]).astype(jnp.float32)
    gk_short = (grad_mixed * v_short).astype(jnp.bfloat16)
    gv_short = (grad_mixed * k_short).astype(jnp.bfloat16)
    x_re = spec_x[0].astype(jnp.float32)
    x_im = spec_x[1].astype(jnp.float32)
    g_re = spec_g[0].astype(jnp.float32)
    g_im = spec_g[1].astype(jnp.float32)
    cross_re = ((g_re * x_re + g_im * x_im) * inv_root).astype(jnp.bfloat16)
    cross_im = ((g_im * x_re - g_re * x_im) * inv_root).astype(jnp.bfloat16)
    grad_filter = inverse_transform(cross_re, cross_im)
    behind = from_behind((gq_short[:rim_rows], gk_short[:rim_rows], gv_short[:rim_rows]), "ctx", -1)
    ext_gq = jnp.concatenate([gq_short, behind[0]], axis=0)
    ext_gk = jnp.concatenate([gk_short, behind[1]], axis=0)
    ext_gv = jnp.concatenate([gv_short, behind[2]], axis=0)
    grad_query = filter_back(ext_gq, short_weight[0], local_rows).astype(jnp.bfloat16)
    grad_key = filter_back(ext_gk, short_weight[1], local_rows).astype(jnp.bfloat16)
    grad_value = filter_back(ext_gv, short_weight[2], local_rows).astype(jnp.bfloat16)
    short_part = jnp.stack(
        [
            weight_terms(gq_short, ext_query, tap_count, local_rows),
            weight_terms(gk_short, ext_key, tap_count, local_rows),
            weight_terms(gv_short, ext_value, tap_count, local_rows),
        ]
    )
    short_total = lax.psum(short_part.astype(jnp.bfloat16), "ctx").astype(jnp.float32)
    grad_short = short_total * inv_root
    return (block_out, grad_query, grad_key, grad_value, grad_short, grad_filter)


def solution(mesh):
    in_specs = (
        P("ctx", "tp"),
        P("ctx", "tp"),
        P("ctx", "tp"),
        P("ctx", "tp"),
        P(None, None, "tp"),
        P("ctx", "tp"),
    )
    out_specs = (
        P("ctx", "tp"),
        P("ctx", "tp"),
        P("ctx", "tp"),
        P("ctx", "tp"),
        P(None, None, "tp"),
        P("ctx", "tp"),
    )
    return jax.shard_map(
        on_device, mesh=mesh, in_specs=in_specs, out_specs=out_specs, check_vma=False
    )
```

profile of v0, /device:TPU:0, one launch (start us, length us, event | category | flops | bytes accessed | tf_op | source)
XLA Modules:
  0.0 1779.4 jit_solution(3266055221568281410)
XLA Ops:
  36.9 24.2 %all-to-all-done.3 = bf16[2,128,4096]{2,0,1:T(2,128)(2,1)} async-done(((bf16[2,128,4096]{2,0,1:T(2,128)(2,1)}), bf16[2,128,4096]{2,0,1:T(2,128)(2,1)}, u32[]{:S(2)}, u32[]{:S(2)}) %all-to-all-start.3) | async-done | bytes 2097184 | tf_op jit(solution)/shard_map/all_to_all | solution.py:120
  61.1 20.4 %all-to-all-start = ((bf16[2,128,4096]{2,0,1:T(2,128)(2,1)}), bf16[2,128,4096]{2,0,1:T(2,128)(2,1)}, u32[]{:S(2)}, u32[]{:S(2)}) async-start(bf16[2,128,4096]{2,0,1:T(2,128)(2,1)} %copy.153), calls=%async_computation | async-start | bytes 4194304 | tf_op jit(solution)/shard_map/all_to_all | solution.py:120
  91.2 31.4 %all-to-all-done = bf16[2,128,4096]{2,0,1:T(2,128)(2,1)} async-done(((bf16[2,128,4096]{2,0,1:T(2,128)(2,1)}), bf16[2,128,4096]{2,0,1:T(2,128)(2,1)}, u32[]{:S(2)}, u32[]{:S(2)}) %all-to-all-start) | async-done | bytes 2097184 | tf_op jit(solution)/shard_map/all_to_all | solution.py:120
  189.1 23.9 %add_convert_fusion.3 = (bf16[64,8,4096]{2,0,1:T(8,128)(2,1)}, bf16[64,8,4096]{2,0,1:T(8,128)(2,1)}, bf16[64,8,4096]{2,0,1:T(8,128)(2,1)}, bf16[64,8,4096]{2,0,1...) fusion(f32[64,8,4096]{2,0,1:T(8,128)} %fusion.91, f32[64,8]{0,1:T(8,128)S(1)} %get-tuple-element.62, ...), kind=kOutput, calls=%fused_computation.43 | convolution fusion | flops 190871552 | bytes 69210112 | tf_op jit(solution)/shard_map/dot_general | solution.py:122
  237.4 71.2 %all-to-all-done.11 = bf16[64,8,4096]{2,1,0:T(8,128)(2,1)} async-done(((bf16[64,8,4096]{2,1,0:T(8,128)(2,1)}), bf16[64,8,4096]{2,1,0:T(8,128)(2,1)}, u32[]{:S(2)}, u32[]{:S(2)}) %all-to-all-start.11) | async-done | bytes 4194336 | tf_op jit(solution)/shard_map/all_to_all | solution.py:132
  334.8 71.1 %all-to-all-done.5 = bf16[64,8,4096]{2,1,0:T(8,128)(2,1)} async-done(((bf16[64,8,4096]{2,1,0:T(8,128)(2,1)}), bf16[64,8,4096]{2,1,0:T(8,128)(2,1)}, u32[]{:S(2)}, u32[]{:S(2)}) %all-to-all-start.5) | async-done | bytes 4194336 | tf_op jit(solution)/shard_map/all_to_all | solution.py:132
  405.9 19.7 %all-to-all-start.4 = ((bf16[64,8,4096]{2,1,0:T(8,128)(2,1)}), bf16[64,8,4096]{2,1,0:T(8,128)(2,1)}, u32[]{:S(2)}, u32[]{:S(2)}) async-start(bf16[64,8,4096]{2,1,0:T(8,128)(2,1)} %copy.169), calls=%async_computation.4 | async-start | bytes 8388608 | tf_op jit(solution)/shard_map/all_to_all | solution.py:131
  432.1 71.2 %all-to-all-done.4 = bf16[64,8,4096]{2,1,0:T(8,128)(2,1)} async-done(((bf16[64,8,4096]{2,1,0:T(8,128)(2,1)}), bf16[64,8,4096]{2,1,0:T(8,128)(2,1)}, u32[]{:S(2)}, u32[]{:S(2)}) %all-to-all-start.4) | async-done | bytes 4194336 | tf_op jit(solution)/shard_map/all_to_all | solution.py:131
  503.3 19.7 %all-to-all-start.2 = ((bf16[64,8,4096]{2,1,0:T(8,128)(2,1)}), bf16[64,8,4096]{2,1,0:T(8,128)(2,1)}, u32[]{:S(2)}, u32[]{:S(2)}) async-start(bf16[64,8,4096]{2,1,0:T(8,128)(2,1)} %copy.161), calls=%async_computation.2 | async-start | bytes 8388608 | tf_op jit(solution)/shard_map/all_to_all | solution.py:132
  529.6 71.1 %all-to-all-done.2 = bf16[64,8,4096]{2,1,0:T(8,128)(2,1)} async-done(((bf16[64,8,4096]{2,1,0:T(8,128)(2,1)}), bf16[64,8,4096]{2,1,0:T(8,128)(2,1)}, u32[]{:S(2)}, u32[]{:S(2)}) %all-to-all-start.2) | async-done | bytes 4194336 | tf_op jit(solution)/shard_map/all_to_all | solution.py:132
  600.7 19.7 %all-to-all-start.1 = ((bf16[64,8,4096]{2,1,0:T(8,128)(2,1)}), bf16[64,8,4096]{2,1,0:T(8,128)(2,1)}, u32[]{:S(2)}, u32[]{:S(2)}) async-start(bf16[64,8,4096]{2,1,0:T(8,128)(2,1)} %copy.158), calls=%async_computation.1 | async-start | bytes 8388608 | tf_op jit(solution)/shard_map/all_to_all | solution.py:131
  626.8 71.2 %all-to-all-done.1 = bf16[64,8,4096]{2,1,0:T(8,128)(2,1)} async-done(((bf16[64,8,4096]{2,1,0:T(8,128)(2,1)}), bf16[64,8,4096]{2,1,0:T(8,128)(2,1)}, u32[]{:S(2)}, u32[]{:S(2)}) %all-to-all-start.1) | async-done | bytes 4194336 | tf_op jit(solution)/shard_map/all_to_all | solution.py:131
  698.1 19.9 %all-to-all-start.10 = ((bf16[64,8,4096]{2,1,0:T(8,128)(2,1)}), bf16[64,8,4096]{2,1,0:T(8,128)(2,1)}, u32[]{:S(2)}, u32[]{:S(2)}) async-start(bf16[64,8,4096]{2,1,0:T(8,128)(2,1)} %copy.191), calls=%async_computation.10 | async-start | bytes 8388608 | tf_op jit(solution)/shard_map/all_to_all | solution.py:131
  769.8 25.6 %all-to-all-done.10 = bf16[64,8,4096]{2,1,0:T(8,128)(2,1)} async-done(((bf16[64,8,4096]{2,1,0:T(8,128)(2,1)}), bf16[64,8,4096]{2,1,0:T(8,128)(2,1)}, u32[]{:S(2)}, u32[]{:S(2)}) %all-to-all-start.10) | async-done | bytes 4194336 | tf_op jit(solution)/shard_map/all_to_all | solution.py:131
  804.9 21.9 %fusion.12 = (bf16[4,128,4096]{1,2,0:T(8,128)(2,1)}, bf16[4,128,4096]{1,2,0:T(8,128)(2,1)}, bf16[4,128,4096]{1,2,0:T(8,128)(2,1)}, bf16[4,128,4096]{1,2,0:T(8,12...) fusion(bf16[4,4096,128]{2,1,0:T(8,128)(2,1)} %add_convert_fusion.2, ...), kind=kOutput, calls=%fused_computation.19 | convolution fusion | flops 610516992 | bytes 58720256 | tf_op jit(solution)/shard_map/js,ksc->kjc/dot_general | solution.py:139
  870.2 28.6 %fusion.51 = (bf16[4,128,4096]{1,2,0:T(8,128)(2,1)}, bf16[4,128,4096]{1,2,0:T(8,128)(2,1)}, bf16[4,128,4096]{1,2,0:T(8,128)(2,1)}, bf16[4,128,4096]{1,2,0:T(8,12...) fusion(f32[4,4096,128]{2,1,0:T(8,128)} %convolution_subtract_fusion.3, ...), kind=kOutput, calls=%fused_computation.114 | convolution fusion | flops 589545472 | bytes 79695872 | tf_op jit(solution)/shard_map/sj,kjc->ksc/dot_general | solution.py:145
  906.7 19.7 %all-to-all-start.16 = ((bf16[4,128,4096]{2,0,1:T(4,128)(2,1)}), bf16[4,128,4096]{2,0,1:T(4,128)(2,1)}, u32[]{:S(2)}, u32[]{:S(2)}) async-start(bf16[4,128,4096]{2,0,1:T(4,128)(2,1)} %copy.209), calls=%async_computation.16 | async-start | bytes 8388608 | tf_op jit(solution)/shard_map/all_to_all | solution.py:153
  934.3 69.8 %all-to-all-done.16 = bf16[4,128,4096]{2,0,1:T(4,128)(2,1)} async-done(((bf16[4,128,4096]{2,0,1:T(4,128)(2,1)}), bf16[4,128,4096]{2,0,1:T(4,128)(2,1)}, u32[]{:S(2)}, u32[]{:S(2)}) %all-to-all-start.16) | async-done | bytes 4194336 | tf_op jit(solution)/shard_map/all_to_all | solution.py:153
  1004.1 19.7 %all-to-all-start.15 = ((bf16[4,128,4096]{2,0,1:T(4,128)(2,1)}), bf16[4,128,4096]{2,0,1:T(4,128)(2,1)}, u32[]{:S(2)}, u32[]{:S(2)}) async-start(bf16[4,128,4096]{2,0,1:T(4,128)(2,1)} %copy.206), calls=%async_computation.15 | async-start | bytes 8388608 | tf_op jit(solution)/shard_map/all_to_all | solution.py:152
  1031.7 69.7 %all-to-all-done.15 = bf16[4,128,4096]{2,0,1:T(4,128)(2,1)} async-done(((bf16[4,128,4096]{2,0,1:T(4,128)(2,1)}), bf16[4,128,4096]{2,0,1:T(4,128)(2,1)}, u32[]{:S(2)}, u32[]{:S(2)}) %all-to-all-start.15) | async-done | bytes 4194336 | tf_op jit(solution)/shard_map/all_to_all | solution.py:152
  1101.5 19.7 %all-to-all-start.6 = ((bf16[4,128,4096]{2,0,1:T(4,128)(2,1)}), bf16[4,128,4096]{2,0,1:T(4,128)(2,1)}, u32[]{:S(2)}, u32[]{:S(2)}) async-start(bf16[4,128,4096]{2,0,1:T(4,128)(2,1)} %copy.179), calls=%async_computation.6 | async-start | bytes 8388608 | tf_op jit(solution)/shard_map/all_to_all | solution.py:152
  1129.1 69.8 %all-to-all-done.6 = bf16[4,128,4096]{2,0,1:T(4,128)(2,1)} async-done(((bf16[4,128,4096]{2,0,1:T(4,128)(2,1)}), bf16[4,128,4096]{2,0,1:T(4,128)(2,1)}, u32[]{:S(2)}, u32[]{:S(2)}) %all-to-all-start.6) | async-done | bytes 4194336 | tf_op jit(solution)/shard_map/all_to_all | solution.py:152
  1198.9 19.7 %all-to-all-start.7 = ((bf16[4,128,4096]{2,0,1:T(4,128)(2,1)}), bf16[4,128,4096]{2,0,1:T(4,128)(2,1)}, u32[]{:S(2)}, u32[]{:S(2)}) async-start(bf16[4,128,4096]{2,0,1:T(4,128)(2,1)} %copy.182), calls=%async_computation.7 | async-start | bytes 8388608 | tf_op jit(solution)/shard_map/all_to_all | solution.py:153
  1226.5 69.7 %all-to-all-done.7 = bf16[4,128,4096]{2,0,1:T(4,128)(2,1)} async-done(((bf16[4,128,4096]{2,0,1:T(4,128)(2,1)}), bf16[4,128,4096]{2,0,1:T(4,128)(2,1)}, u32[]{:S(2)}, u32[]{:S(2)}) %all-to-all-start.7) | async-done | bytes 4194336 | tf_op jit(solution)/shard_map/all_to_all | solution.py:153
  1296.2 19.7 %all-to-all-start.12 = ((bf16[4,128,4096]{2,0,1:T(4,128)(2,1)}), bf16[4,128,4096]{2,0,1:T(4,128)(2,1)}, u32[]{:S(2)}, u32[]{:S(2)}) async-start(bf16[4,128,4096]{2,0,1:T(4,128)(2,1)} %copy.199), calls=%async_computation.12 | async-start | bytes 8388608 | tf_op jit(solution)/shard_map/all_to_all | solution.py:152
  1323.9 69.7 %all-to-all-done.12 = bf16[4,128,4096]{2,0,1:T(4,128)(2,1)} async-done(((bf16[4,128,4096]{2,0,1:T(4,128)(2,1)}), bf16[4,128,4096]{2,0,1:T(4,128)(2,1)}, u32[]{:S(2)}, u32[]{:S(2)}) %all-to-all-start.12) | async-done | bytes 4194336 | tf_op jit(solution)/shard_map/all_to_all | solution.py:152
  1393.6 20.1 %all-to-all-start.13 = ((bf16[4,128,4096]{2,0,1:T(4,128)(2,1)}), bf16[4,128,4096]{2,0,1:T(4,128)(2,1)}, u32[]{:S(2)}, u32[]{:S(2)}) async-start(bf16[4,128,4096]{2,0,1:T(4,128)(2,1)} %copy.202), calls=%async_computation.13 | async-start | bytes 8388608 | tf_op jit(solution)/shard_map/all_to_all | solution.py:153
  1433.3 57.6 %all-to-all-done.13 = bf16[4,128,4096]{2,0,1:T(4,128)(2,1)} async-done(((bf16[4,128,4096]{2,0,1:T(4,128)(2,1)}), bf16[4,128,4096]{2,0,1:T(4,128)(2,1)}, u32[]{:S(2)}, u32[]{:S(2)}) %all-to-all-start.13) | async-done | bytes 4194336 | tf_op jit(solution)/shard_map/all_to_all | solution.py:153
  1530.3 21.4 %all-to-all-done.17 = bf16[32,8,4096]{2,1,0:T(8,128)(2,1)S(1)} async-done(((bf16[32,8,4096]{2,1,0:T(8,128)(2,1)}), bf16[32,8,4096]{2,1,0:T(8,128)(2,1)S(1)}, u32[]{:S(2)}, u32[]{:S(2)}) %all-to-all-start.17) | async-done | bytes 2097184 | tf_op jit(solution)/shard_map/all_to_all | solution.py:169
  1584.0 21.4 %all-to-all-done.8 = bf16[32,8,4096]{2,1,0:T(8,128)(2,1)S(1)} async-done(((bf16[32,8,4096]{2,1,0:T(8,128)(2,1)}), bf16[32,8,4096]{2,1,0:T(8,128)(2,1)S(1)}, u32[]{:S(2)}, u32[]{:S(2)}) %all-to-all-start.8) | async-done | bytes 2097184 | tf_op jit(solution)/shard_map/all_to_all | solution.py:169
  1629.1 28.7 %all-to-all-done.14 = bf16[32,8,4096]{2,1,0:T(8,128)(2,1)} async-done(((bf16[32,8,4096]{2,1,0:T(8,128)(2,1)}), bf16[32,8,4096]{2,1,0:T(8,128)(2,1)}, u32[]{:S(2)}, u32[]{:S(2)}) %all-to-all-start.14) | async-done | bytes 2097184 | tf_op jit(solution)/shard_map/all_to_all | solution.py:169
  1684.9 85.7 %all-reduce.2.cloned.1.call-done = bf16[3,3,4096]{2,1,0:T(4,128)(2,1)} async-done(((bf16[3,3,4096]{2,1,0:T(4,128)(2,1)}), bf16[3,3,4096]{2,1,0:T(4,128)(2,1)}) %all-reduce.2.cloned.1.call-update) | async-done | bytes 73744 | tf_op jit(solution)/shard_map/psum | solution.py:208
  (209 shorter events, 471.1 us)
Async XLA Ops:
  12.4 48.6 %all-to-all-start.3 = ((bf16[2,128,4096]{2,0,1:T(2,128)(2,1)}), bf16[2,128,4096]{2,0,1:T(2,128)(2,1)}, u32[]{:S(2)}, u32[]{:S(2)}) async-start(bf16[2,128,4096]{2,0,1:T(2,128)(2,1)} %copy.164), calls=%async_computation.3 | async-start | bytes 4194304 | tf_op jit(solution)/shard_map/all_to_all | solution.py:120
  19.9 6.9 collective-permute-start.2
  23.1 4.4 collective-permute-start.1
  26.8 57.8 %copy-start.18 = (f32[1,1,4096]{2,1,0:T(1,128)}, f32[1,1,4096]{2,1,0:T(1,128)S(1)}, u32[]{:S(2)}) copy-start(f32[1,1,4096]{2,1,0:T(1,128)S(1)} %get-tuple-element.41) | copy-start | bytes 49156
  26.8 57.8 %copy-start.20 = (f32[1,1,4096]{2,1,0:T(1,128)}, f32[1,1,4096]{2,1,0:T(1,128)S(1)}, u32[]{:S(2)}) copy-start(f32[1,1,4096]{2,1,0:T(1,128)S(1)} %get-tuple-element.46) | copy-start | bytes 49156
  26.8 57.8 %copy-start.22 = (f32[1,1,4096]{2,1,0:T(1,128)}, f32[1,1,4096]{2,1,0:T(1,128)S(1)}, u32[]{:S(2)}) copy-start(f32[1,1,4096]{2,1,0:T(1,128)S(1)} %get-tuple-element.47) | copy-start | bytes 49156
  33.4 48.1 %copy-start.6 = (bf16[256,4096]{1,0:T(8,128)(2,1)S(1)}, bf16[256,4096]{1,0:T(8,128)(2,1)}, u32[]{:S(2)}) copy-start(bf16[256,4096]{1,0:T(8,128)(2,1)} %param.6) | copy-start | bytes 6291460
  61.1 61.6 %all-to-all-start = ((bf16[2,128,4096]{2,0,1:T(2,128)(2,1)}), bf16[2,128,4096]{2,0,1:T(2,128)(2,1)}, u32[]{:S(2)}, u32[]{:S(2)}) async-start(bf16[2,128,4096]{2,0,1:T(2,128)(2,1)} %copy.153), calls=%async_computation | async-start | bytes 4194304 | tf_op jit(solution)/shard_map/all_to_all | solution.py:120
  81.5 3.1 collective-permute-start
  122.6 58.3 %all-to-all-start.9 = ((bf16[2,128,4096]{2,0,1:T(2,128)(2,1)}), bf16[2,128,4096]{2,0,1:T(2,128)(2,1)S(1)}, u32[]{:S(2)}, u32[]{:S(2)}) async-start(bf16[2,128,4096]{2,0,1:T(2,128)(2,1)} %copy.186), calls=%async_computation.9 | async-start | bytes 4194304 | tf_op jit(solution)/shard_map/all_to_all | solution.py:120
  219.5 89.1 %all-to-all-start.11 = ((bf16[64,8,4096]{2,1,0:T(8,128)(2,1)}), bf16[64,8,4096]{2,1,0:T(8,128)(2,1)}, u32[]{:S(2)}, u32[]{:S(2)}) async-start(bf16[64,8,4096]{2,1,0:T(8,128)(2,1)} %copy.194), calls=%async_computation.11 | async-start | bytes 8388608 | tf_op jit(solution)/shard_map/all_to_all | solution.py:132
  308.6 97.4 %all-to-all-start.5 = ((bf16[64,8,4096]{2,1,0:T(8,128)(2,1)}), bf16[64,8,4096]{2,1,0:T(8,128)(2,1)}, u32[]{:S(2)}, u32[]{:S(2)}) async-start(bf16[64,8,4096]{2,1,0:T(8,128)(2,1)} %copy.172), calls=%async_computation.5 | async-start | bytes 8388608 | tf_op jit(solution)/shard_map/all_to_all | solution.py:132
  405.9 97.4 %all-to-all-start.4 = ((bf16[64,8,4096]{2,1,0:T(8,128)(2,1)}), bf16[64,8,4096]{2,1,0:T(8,128)(2,1)}, u32[]{:S(2)}, u32[]{:S(2)}) async-start(bf16[64,8,4096]{2,1,0:T(8,128)(2,1)} %copy.169), calls=%async_computation.4 | async-start | bytes 8388608 | tf_op jit(solution)/shard_map/all_to_all | solution.py:131
  503.3 97.4 %all-to-all-start.2 = ((bf16[64,8,4096]{2,1,0:T(8,128)(2,1)}), bf16[64,8,4096]{2,1,0:T(8,128)(2,1)}, u32[]{:S(2)}, u32[]{:S(2)}) async-start(bf16[64,8,4096]{2,1,0:T(8,128)(2,1)} %copy.161), calls=%async_computation.2 | async-start | bytes 8388608 | tf_op jit(solution)/shard_map/all_to_all | solution.py:132
  600.7 97.4 %all-to-all-start.1 = ((bf16[64,8,4096]{2,1,0:T(8,128)(2,1)}), bf16[64,8,4096]{2,1,0:T(8,128)(2,1)}, u32[]{:S(2)}, u32[]{:S(2)}) async-start(bf16[64,8,4096]{2,1,0:T(8,128)(2,1)} %copy.158), calls=%async_computation.1 | async-start | bytes 8388608 | tf_op jit(solution)/shard_map/all_to_all | solution.py:131
  698.1 97.4 %all-to-all-start.10 = ((bf16[64,8,4096]{2,1,0:T(8,128)(2,1)}), bf16[64,8,4096]{2,1,0:T(8,128)(2,1)}, u32[]{:S(2)}, u32[]{:S(2)}) async-start(bf16[64,8,4096]{2,1,0:T(8,128)(2,1)} %copy.191), calls=%async_computation.10 | async-start | bytes 8388608 | tf_op jit(solution)/shard_map/all_to_all | solution.py:131
  906.7 97.4 %all-to-all-start.16 = ((bf16[4,128,4096]{2,0,1:T(4,128)(2,1)}), bf16[4,128,4096]{2,0,1:T(4,128)(2,1)}, u32[]{:S(2)}, u32[]{:S(2)}) async-start(bf16[4,128,4096]{2,0,1:T(4,128)(2,1)} %copy.209), calls=%async_computation.16 | async-start | bytes 8388608 | tf_op jit(solution)/shard_map/all_to_all | solution.py:153
  1004.1 97.4 %all-to-all-start.15 = ((bf16[4,128,4096]{2,0,1:T(4,128)(2,1)}), bf16[4,128,4096]{2,0,1:T(4,128)(2,1)}, u32[]{:S(2)}, u32[]{:S(2)}) async-start(bf16[4,128,4096]{2,0,1:T(4,128)(2,1)} %copy.206), calls=%async_computation.15 | async-start | bytes 8388608 | tf_op jit(solution)/shard_map/all_to_all | solution.py:152
  1101.5 97.4 %all-to-all-start.6 = ((bf16[4,128,4096]{2,0,1:T(4,128)(2,1)}), bf16[4,128,4096]{2,0,1:T(4,128)(2,1)}, u32[]{:S(2)}, u32[]{:S(2)}) async-start(bf16[4,128,4096]{2,0,1:T(4,128)(2,1)} %copy.179), calls=%async_computation.6 | async-start | bytes 8388608 | tf_op jit(solution)/shard_map/all_to_all | solution.py:152
  1198.9 97.4 %all-to-all-start.7 = ((bf16[4,128,4096]{2,0,1:T(4,128)(2,1)}), bf16[4,128,4096]{2,0,1:T(4,128)(2,1)}, u32[]{:S(2)}, u32[]{:S(2)}) async-start(bf16[4,128,4096]{2,0,1:T(4,128)(2,1)} %copy.182), calls=%async_computation.7 | async-start | bytes 8388608 | tf_op jit(solution)/shard_map/all_to_all | solution.py:153
  1296.2 97.4 %all-to-all-start.12 = ((bf16[4,128,4096]{2,0,1:T(4,128)(2,1)}), bf16[4,128,4096]{2,0,1:T(4,128)(2,1)}, u32[]{:S(2)}, u32[]{:S(2)}) async-start(bf16[4,128,4096]{2,0,1:T(4,128)(2,1)} %copy.199), calls=%async_computation.12 | async-start | bytes 8388608 | tf_op jit(solution)/shard_map/all_to_all | solution.py:152
  1393.6 97.4 %all-to-all-start.13 = ((bf16[4,128,4096]{2,0,1:T(4,128)(2,1)}), bf16[4,128,4096]{2,0,1:T(4,128)(2,1)}, u32[]{:S(2)}, u32[]{:S(2)}) async-start(bf16[4,128,4096]{2,0,1:T(4,128)(2,1)} %copy.202), calls=%async_computation.13 | async-start | bytes 8388608 | tf_op jit(solution)/shard_map/all_to_all | solution.py:153
  1491.0 60.8 %all-to-all-start.17 = ((bf16[32,8,4096]{2,1,0:T(8,128)(2,1)}), bf16[32,8,4096]{2,1,0:T(8,128)(2,1)S(1)}, u32[]{:S(2)}, u32[]{:S(2)}) async-start(bf16[32,8,4096]{2,1,0:T(8,128)(2,1)} %bitcast.392), calls=%async_computation.17 | async-start | bytes 4194304 | tf_op jit(solution)/shard_map/all_to_all | solution.py:169
  1553.1 52.3 %all-to-all-start.8 = ((bf16[32,8,4096]{2,1,0:T(8,128)(2,1)}), bf16[32,8,4096]{2,1,0:T(8,128)(2,1)S(1)}, u32[]{:S(2)}, u32[]{:S(2)}) async-start(bf16[32,8,4096]{2,1,0:T(8,128)(2,1)} %bitcast.393), calls=%async_computation.8 | async-start | bytes 4194304 | tf_op jit(solution)/shard_map/all_to_all | solution.py:169
  1605.4 52.4 %all-to-all-start.14 = ((bf16[32,8,4096]{2,1,0:T(8,128)(2,1)}), bf16[32,8,4096]{2,1,0:T(8,128)(2,1)}, u32[]{:S(2)}, u32[]{:S(2)}) async-start(bf16[32,8,4096]{2,1,0:T(8,128)(2,1)} %bitcast.394), calls=%async_computation.14 | async-start | bytes 4194304 | tf_op jit(solution)/shard_map/all_to_all | solution.py:169
  1616.7 153.9 %all-reduce.2.cloned.1.call-start = ((), (), s32[]{:S(2)}) async-start(), calls=%async_computation.18 | async-start | bytes 196608 | tf_op jit(solution)/shard_map/psum | solution.py:208
  1626.3 33.8 %copy-start.13 = (f32[1,1,4096]{2,1,0:T(1,128)S(1)}, f32[1,1,4096]{2,1,0:T(1,128)}, u32[]{:S(2)}) copy-start(f32[1,1,4096]{2,1,0:T(1,128)} %copy-done.12) | copy-start | bytes 49156
  1626.3 33.8 %copy-start.15 = (f32[1,1,4096]{2,1,0:T(1,128)S(1)}, f32[1,1,4096]{2,1,0:T(1,128)}, u32[]{:S(2)}) copy-start(f32[1,1,4096]{2,1,0:T(1,128)} %copy-done.14) | copy-start | bytes 49156
  1626.3 33.8 %copy-start.17 = (f32[1,1,4096]{2,1,0:T(1,128)S(1)}, f32[1,1,4096]{2,1,0:T(1,128)}, u32[]{:S(2)}) copy-start(f32[1,1,4096]{2,1,0:T(1,128)} %copy-done.16) | copy-start | bytes 49156
  1627.6 49.5 %collective-permute-start.3 = (bf16[2,4096]{1,0:T(2,128)(2,1)S(1)}, bf16[2,4096]{1,0:T(2,128)(2,1)S(1)}, u32[]{:S(2)}, u32[]{:S(2)}) collective-permute-start(bf16[2,4096]{1,0:T(2,128)(2,1)S(1)} %slice.153), channel_id=1, source_target_pairs={{2,0},{4,2},{6,4},{8,6},{10,8},{12,10},{14,12},{16,14},{18,16},{20... | collective-permute-start | bytes 49160 | tf_op jit(solution)/shard_map/ppermute | solution.py:14
  1664.1 3.3 collective-permute-start.5
  1675.8 6.3 collective-permute-start.4
  (32 other events, 260.4 us)
Sparse Core Ops, SparseCore 0:
  1675.1 95.4 all-reduce.1
where the time goes:
time: 1790 us; the launch traced here: 1780 us
  waiting for transfers between devices  1010 us (56%)
  starting transfers between devices  328 us (18%)
  matrix products  217 us (12%)
  local copies, waits for them, and re-layouts  173 us (10%)
  other arithmetic  34.7 us (2%)
    all_to_all x3, waiting for transfers between devices, forward_transform(): lax.all_to_all(twist_im, 'ctx', split_axis=0, concat_axis=1, tiled=True)  213 us
    all_to_all x3, waiting for transfers between devices, inverse_transform(): lax.all_to_all(untw_re, 'ctx', split_axis=1, concat_axis=0, tiled=True)  209 us
    all_to_all x3, waiting for transfers between devices, inverse_transform(): lax.all_to_all(untw_im, 'ctx', split_axis=1, concat_axis=0, tiled=True)  197 us
    all_to_all x3, waiting for transfers between devices, forward_transform(): lax.all_to_all(twist_re, 'ctx', split_axis=0, concat_axis=1, tiled=True)  168 us
    psum x1, waiting for transfers between devices, on_device(): lax.psum(short_part.astype(jnp.bfloat16), 'ctx').astype(jnp.float32)  85.7 us
    all_to_all x3, waiting for transfers between devices, inverse_transform(): lax.all_to_all(signal, 'ctx', split_axis=0, concat_axis=1, tiled=True)  71.6 us
    all_to_all x3, waiting for transfers between devices, forward_transform(): lax.all_to_all(grid_rows, 'ctx', split_axis=1, concat_axis=0, tiled=True)  63.2 us
    all_to_all x3, starting transfers between devices, inverse_transform(): lax.all_to_all(untw_im, 'ctx', split_axis=1, concat_axis=0, tiled=True)  59.5 us
  transfers between devices with their start and end apart: 25, of which 22 were waited for; matrix products, arithmetic and copies ran while one was open for 15% of the time, Pallas kernels for 0%

commit v1 on v0

v1 whole, which is shorter than its diff:
```python
import functools
import math

import jax
import jax.numpy as jnp
import numpy as np
from jax import lax
from jax.experimental import pallas as pl
from jax.experimental.pallas import tpu as pltpu
from jax.sharding import PartitionSpec as P

S = 128
G = 16
LANES = 128


def from_behind(x, axis, by):
    count = lax.axis_size(axis)
    pairs = [(i, i + by) for i in range(count) if 0 <= i + by < count]
    return lax.ppermute(x, axis, pairs)


def short_filter(extended, weights, local_rows):
    tap_count = weights.shape[0]
    result = jnp.zeros((local_rows, extended.shape[1]), jnp.float32)
    for lag_index in range(tap_count):
        offset_row = tap_count - 1 - lag_index
        result = result + weights[lag_index] * extended[
            offset_row : offset_row + local_rows
        ].astype(jnp.float32)
    return result


def filter_back(extended, weights, local_rows):
    tap_count = weights.shape[0]
    result = jnp.zeros((local_rows, extended.shape[1]), jnp.float32)
    for lag_index in range(tap_count):
        result = result + weights[lag_index] * extended[lag_index : lag_index + local_rows].astype(
            jnp.float32
        )
    return result


def weight_terms(grads, extended, tap_count, local_rows):
    grad_float = grads.astype(jnp.float32)
    terms = []
    for lag_index in range(tap_count):
        offset_row = tap_count - 1 - lag_index
        terms.append(
            jnp.sum(
                grad_float * extended[offset_row : offset_row + local_rows].astype(jnp.float32),
                axis=0,
            )
        )
    return jnp.stack(terms)


def grid_tables(outer_len):
    half_rows = outer_len // 2
    k_count = half_rows + 1
    k_ids = np.arange(k_count)[:, None]
    r_ids = np.arange(half_rows)[None, :]
    angle = 2.0 * np.pi / outer_len * (k_ids * r_ids % outer_len)
    first = np.concatenate([np.cos(angle), -np.sin(angle)[1:half_rows]], axis=0)
    weight = np.full((k_count, 1), 2.0)
    weight[0] = weight[half_rows] = 1.0
    back = np.concatenate([weight * np.cos(angle), -2.0 * np.sin(angle)[1:half_rows]], axis=0).T
    inner = 2.0 * np.pi / S * (np.arange(S)[:, None] * np.arange(S)[None, :] % S)
    cos, sin = np.cos(inner), np.sin(inner)
    inner_fwd = np.block([[cos, sin], [-sin, cos]])
    inner_back = np.block([[cos, -sin], [sin, cos]])
    turn = 2.0 * np.pi / (outer_len * S) * (k_ids * np.arange(S)[None, :])
    return first, back, inner_fwd, inner_back, np.cos(turn), np.sin(turn)


def spread_over_rows(table):
    return jnp.asarray(np.kron(table, np.eye(G)).astype(jnp.bfloat16))


def spectral_kernel(
    inv_root,
    scale,
    xg_ref,
    h_ref,
    first_ref,
    back_ref,
    inner_fwd_ref,
    inner_back_ref,
    cos_ref,
    sin_ref,
    cg_ref,
    gf_ref,
    work,
):
    k_count = work.shape[0]
    half_rows = k_count - 1
    rows_per = h_ref.shape[1] // S

    def first_section(step, carry):
        at = pl.multiple_of(step * G, G)
        pieces = []
        for r in range(half_rows):
            rows = pl.ds((r % rows_per) * S + at, G)
            pieces.append(
                jnp.concatenate(
                    [
                        xg_ref[r // rows_per, 0, rows, :],
                        xg_ref[r // rows_per, 1, rows, :],
                        h_ref[r // rows_per, rows, :],
                    ],
                    axis=1,
                )
            )
        grid_rows = jnp.concatenate(pieces, axis=0)
        first = jnp.dot(first_ref[...], grid_rows, preferred_element_type=jnp.float32)
        for k in range(k_count):
            re = first[k * G : (k + 1) * G]
            cos = jnp.concatenate([cos_ref[k, pl.ds(at, G), :]] * 3, axis=1)
            sin = jnp.concatenate([sin_ref[k, pl.ds(at, G), :]] * 3, axis=1)
            if 0 < k < half_rows:
                row = (k_count + k - 1) * G
                im = first[row : row + G]
                turned_re = re * cos + im * sin
                turned_im = im * cos - re * sin
            else:
                turned_re = re * cos
                turned_im = -re * sin
            work[k, pl.ds(at, G), :] = turned_re.astype(jnp.bfloat16)
            work[k, pl.ds(S + at, G), :] = turned_im.astype(jnp.bfloat16)
        return carry

    lax.fori_loop(0, S // G, first_section, 0)

    def one_row(k):
        spec = jnp.dot(inner_fwd_ref[...], work[k], preferred_element_type=jnp.float32)
        spec = spec.astype(jnp.bfloat16).astype(jnp.float32)
        x_re, x_im = spec[:S, :LANES], spec[S:, :LANES]
        g_re, g_im = spec[:S, LANES : 2 * LANES], spec[S:, LANES : 2 * LANES]
        h_re, h_im = spec[:S, 2 * LANES :], spec[S:, 2 * LANES :]
        real = jnp.concatenate(
            [
                x_re * h_re - x_im * h_im,
                g_re * h_re + g_im * h_im,
                (g_re * x_re + g_im * x_im) * inv_root,
            ],
            axis=1,
        )
        imag = jnp.concatenate(
            [
                x_re * h_im + x_im * h_re,
                g_im * h_re - g_re * h_im,
                (g_im * x_re - g_re * x_im) * inv_root,
            ],
            axis=1,
        )
        product = jnp.concatenate([real, imag], axis=0).astype(jnp.bfloat16)
        back = jnp.dot(inner_back_ref[...], product, preferred_element_type=jnp.float32)
        cos = jnp.concatenate([cos_ref[k]] * 3, axis=1)
        sin = jnp.concatenate([sin_ref[k]] * 3, axis=1)
        work[k, :S, :] = (back[:S] * cos - back[S:] * sin).astype(jnp.bfloat16)
        work[k, S:, :] = (back[S:] * cos + back[:S] * sin).astype(jnp.bfloat16)

    batch = next(n for n in (3, 5, 1) if k_count % n == 0)

    def some_rows(step, carry):
        for i in range(batch):
            one_row(step * batch + i)
        return carry

    lax.fori_loop(0, k_count // batch, some_rows, 0)

    def last_section(step, carry):
        at = pl.multiple_of(step * G, G)
        pieces = [work[k, pl.ds(at, G), :] for k in range(k_count)]
        pieces += [work[k, pl.ds(S + at, G), :] for k in range(1, half_rows)]
        signal = jnp.dot(
            back_ref[...], jnp.concatenate(pieces, axis=0), preferred_element_type=jnp.float32
        )
        signal = (signal * scale).astype(jnp.bfloat16)
        for r in range(half_rows):
            rows = pl.ds((r % rows_per) * S + at, G)
            part = signal[r * G : (r + 1) * G]
            cg_ref[r // rows_per, 0, rows, :] = part[:, :LANES]
            cg_ref[r // rows_per, 1, rows, :] = part[:, LANES : 2 * LANES]
            gf_ref[r // rows_per, rows, :] = part[:, 2 * LANES :]
        return carry

    lax.fori_loop(0, S // G, last_section, 0)


def transform_chunk(xg, h, tables, inv_root, scale):
    k_count = tables[4].shape[0]
    lanes = h.shape[-1]
    if lanes < LANES:
        xg = jnp.pad(xg, ((0, 0),) * 3 + ((0, LANES - lanes),))
        h = jnp.pad(h, ((0, 0),) * 2 + ((0, LANES - lanes),))
    cg, gf = pl.pallas_call(
        functools.partial(spectral_kernel, inv_root, scale),
        out_shape=(
            jax.ShapeDtypeStruct(xg.shape, jnp.bfloat16),
            jax.ShapeDtypeStruct(h.shape, jnp.bfloat16),
        ),
        in_specs=[pl.BlockSpec(memory_space=pltpu.VMEM)] * 8,
        out_specs=(pl.BlockSpec(memory_space=pltpu.VMEM),) * 2,
        scratch_shapes=[pltpu.VMEM((k_count, 2 * S, 3 * LANES), jnp.bfloat16)],
        compiler_params=pltpu.CompilerParams(vmem_limit_bytes=58 * 1024 * 1024),
        cost_estimate=pl.CostEstimate(
            flops=13_000_000_000, bytes_accessed=16_000_000, transcendentals=0
        ),
    )(xg, h, *tables)
    return cg[..., :lanes], gf[..., :lanes]


def exchange(x):
    return lax.all_to_all(x, "ctx", split_axis=0, concat_axis=0, tiled=True)


def sum_over(x, axis):
    count = lax.axis_size(axis)
    step = 1
    while step < count:
        x = x + lax.ppermute(x, axis, [(i, i ^ step) for i in range(count)])
        step *= 2
    return x


def on_device(query_in, key_in, value_in, cotangent, short_weight, long_filter):
    local_rows, channels = query_in.shape
    tap_count = short_weight.shape[1]
    rim_rows = tap_count - 1
    ctx_size = lax.axis_size("ctx")
    length = local_rows * ctx_size
    fft_size = 2 * length
    outer_len = fft_size // S
    inv_root = 1.0 / math.sqrt(length)
    own = channels // ctx_size
    lanes = min(own, LANES)
    chunks = own // lanes

    def to_owners(x):
        return x.reshape(local_rows, ctx_size, chunks, lanes).transpose(2, 1, 0, 3)

    def from_owners(parts):
        return jnp.stack(parts).transpose(2, 1, 0, 3).reshape(local_rows, channels)

    first, back, inner_fwd, inner_back, turn_cos, turn_sin = grid_tables(outer_len)
    tables = (
        spread_over_rows(first),
        spread_over_rows(back),
        jnp.asarray(inner_fwd, jnp.bfloat16),
        jnp.asarray(inner_back, jnp.bfloat16),
        jnp.broadcast_to(
            jnp.asarray(turn_cos, jnp.float32)[:, :, None], turn_cos.shape + (LANES,)
        ),
        jnp.broadcast_to(
            jnp.asarray(turn_sin, jnp.float32)[:, :, None], turn_sin.shape + (LANES,)
        ),
    )
    filter_parts = to_owners(long_filter)
    h_parts = [exchange(filter_parts[c]) for c in range(chunks)]
    ahead = from_behind(
        (
            query_in[local_rows - rim_rows :],
            key_in[local_rows - rim_rows :],
            value_in[local_rows - rim_rows :],
        ),
        "ctx",
        1,
    )
    ext_query = jnp.concatenate([ahead[0], query_in], axis=0)
    ext_key = jnp.concatenate([ahead[1], key_in], axis=0)
    ext_value = jnp.concatenate([ahead[2], value_in], axis=0)
    q_short = short_filter(ext_query, short_weight[0], local_rows)
    k_short = short_filter(ext_key, short_weight[1], local_rows)
    v_short = short_filter(ext_value, short_weight[2], local_rows)
    mixed = (k_short * v_short).astype(jnp.bfloat16)
    cot_float = cotangent.astype(jnp.float32)
    grad_conv = (cot_float * q_short).astype(jnp.bfloat16)
    xg_parts = jnp.stack([to_owners(mixed), to_owners(grad_conv)], axis=2)
    xg_parts = [exchange(xg_parts[c]) for c in range(chunks)]
    cg_parts, gf_parts = [], []
    for xg, h in zip(xg_parts, h_parts):
        cg, gf = transform_chunk(xg, h, tables, inv_root, 1.0 / fft_size)
        cg_parts.append(exchange(cg))
        gf_parts.append(gf)
    gf_parts = [exchange(gf) for gf in gf_parts]
    conv = from_owners([part[:, 0] for part in cg_parts]).astype(jnp.float32)
    grad_mixed = from_owners([part[:, 1] for part in cg_parts]).astype(jnp.float32)
    grad_filter = from_owners(gf_parts)
    block_out = (q_short * conv).astype(jnp.bfloat16)
    gq_short = (cot_float * conv).astype(jnp.bfloat16)
    gk_short = (grad_mixed * v_short).astype(jnp.bfloat16)
    gv_short = (grad_mixed * k_short).astype(jnp.bfloat16)
    behind = from_behind((gq_short[:rim_rows], gk_short[:rim_rows], gv_short[:rim_rows]), "ctx", -1)
    ext_gq = jnp.concatenate([gq_short, behind[0]], axis=0)
    ext_gk = jnp.concatenate([gk_short, behind[1]], axis=0)
    ext_gv = jnp.concatenate([gv_short, behind[2]], axis=0)
    grad_query = filter_back(ext_gq, short_weight[0], local_rows).astype(jnp.bfloat16)
    grad_key = filter_back(ext_gk, short_weight[1], local_rows).astype(jnp.bfloat16)
    grad_value = filter_back(ext_gv, short_weight[2], local_rows).astype(jnp.bfloat16)
    short_part = jnp.stack(
        [
            weight_terms(gq_short, ext_query, tap_count, local_rows),
            weight_terms(gk_short, ext_key, tap_count, local_rows),
            weight_terms(gv_short, ext_value, tap_count, local_rows),
        ]
    )
    grad_short = sum_over(short_part, "ctx") * inv_root
    return (block_out, grad_query, grad_key, grad_value, grad_short, grad_filter)


def solution(mesh):
    in_specs = (
        P("ctx", "tp"),
        P("ctx", "tp"),
        P("ctx", "tp"),
        P("ctx", "tp"),
        P(None, None, "tp"),
        P("ctx", "tp"),
    )
    out_specs = (
        P("ctx", "tp"),
        P("ctx", "tp"),
        P("ctx", "tp"),
        P("ctx", "tp"),
        P(None, None, "tp"),
        P("ctx", "tp"),
    )
    return jax.shard_map(
        on_device, mesh=mesh, in_specs=in_specs, out_specs=out_specs, check_vma=False
    )
```

time: 1790 us -> 433 us (0.24)
  waiting for transfers between devices: 1010 us -> 59 us
  starting transfers between devices: 328 us -> 79.7 us
  matrix products: 217 us -> 0 us
  local copies, waits for them, and re-layouts: 173 us -> 93 us
  Pallas kernels: 0 us -> 57.6 us
  blocking collectives: 0 us -> 53.4 us
  other arithmetic: 34.7 us -> 86.5 us
    all_to_all x18 -> x7, waiting for transfers between devices: 923 us -> 58.8 us  [exchange(): return lax.all_to_all(x, 'ctx', split_axis=0, concat_axis=0, tiled=True)]
    all_to_all x18 -> x7, starting transfers between devices: 316 us -> 59.4 us  [exchange(): return lax.all_to_all(x, 'ctx', split_axis=0, concat_axis=0, tiled=True)]
    dot_general x36 -> x0, matrix products: 217 us -> none  [the longest x3 40.5 us: inverse_transform(): jnp.einsum('sj,kjc->ksc', sin_inner, spec_im, preferred_element_type=jnp....]
    psum x1 -> x0, waiting for transfers between devices: 85.7 us -> none  [on_device(): lax.psum(short_part.astype(jnp.bfloat16), 'ctx').astype(jnp.float32)]
    convert_element_type x14 -> x2, local copies, waits for them, and re-layouts: 89.3 us -> 10.8 us  [the longest x1 5.43 us: on_device(): from_owners([part[:, 1] for part in cg_parts]).astype(jnp.float32)]
    pallas_call x0 -> x2, Pallas kernels: none -> 57.6 us  [transform_chunk(): pl.pallas_call(functools.partial(spectral_kernel, inv_root, scale), out_s...]
    all_to_all x0 -> x1, blocking collectives: none -> 53.4 us  [exchange(): return lax.all_to_all(x, 'ctx', split_axis=0, concat_axis=0, tiled=True)]
    all_to_all x19 -> x0, local copies, waits for them, and re-layouts: 40.8 us -> none  [the longest x6 14.9 us: inverse_transform(): lax.all_to_all(untw_im, 'ctx', split_axis=1, concat_axis=0, tiled=True)]
  transfers between devices with their start and end apart: 25 -> 17, of which waited for: 22 -> 4; matrix products, arithmetic and copies ran while one was open for 15% -> 39% of each run, Pallas kernels for 0% -> 13%
where the time goes in v1:
time: 433 us; the launch traced here: 430 us
  local copies, waits for them, and re-layouts  93 us (21%)
  other arithmetic  86.5 us (20%)
  starting transfers between devices  79.7 us (18%)
  waiting for transfers between devices  59 us (14%)
  Pallas kernels  57.6 us (13%)
  blocking collectives  53.4 us (12%)
    all_to_all x7, starting transfers between devices, exchange(): return lax.all_to_all(x, 'ctx', split_axis=0, concat_axis=0, tiled=True)  59.4 us
    all_to_all x7, waiting for transfers between devices, exchange(): return lax.all_to_all(x, 'ctx', split_axis=0, concat_axis=0, tiled=True)  58.8 us
    pallas_call x2, Pallas kernels, transform_chunk(): pl.pallas_call(functools.partial(spectral_kernel, inv_root, scale), out_s...  57.6 us
    all_to_all x1, blocking collectives, exchange(): return lax.all_to_all(x, 'ctx', split_axis=0, concat_axis=0, tiled=True)  53.4 us
    unnamed x40, local copies, waits for them, and re-layouts  40.6 us
    reduce_sum x3, other arithmetic, weight_terms(): jnp.sum(grad_float * extended[offset_row:offset_row + local_rows].astype(...  40.2 us
    ppermute x6, starting transfers between devices, from_behind(): return lax.ppermute(x, axis, pairs)  11.9 us
    reshape x3, local copies, waits for them, and re-layouts, to_owners(): return x.reshape(local_rows, ctx_size, chunks, lanes).transpose(2, 1, 0, 3)  10.9 us
  transfers between devices with their start and end apart: 17, of which 4 were waited for; matrix products, arithmetic and copies ran while one was open for 39% of the time, Pallas kernels for 13%

profile of v1, /device:TPU:0, one launch (start us, length us, event | category | flops | bytes accessed | tf_op | source)
XLA Modules:
  0.0 430.2 jit_solution(176601007616086574)
XLA Ops:
  0.6 4.1 copy.56
  9.3 7.4 %all-to-all-start.1 = ((bf16[16,256,128]{2,1,0:T(8,128)(2,1)}), bf16[16,256,128]{2,1,0:T(8,128)(2,1)}, u32[]{:S(2)}, u32[]{:S(2)}) async-start(bf16[16,256,128]{2,1,0:T(8,128)(2,1)} %get-tuple-element.47), calls=%async_computation.1 | async-start | bytes 2097152 | tf_op jit(solution)/shard_map/all_to_all | solution.py:215
  31.3 4.1 copy.50
  35.4 4.1 copy.44
  39.4 4.1 copy.54
  45.4 5.7 %all-to-all-start.4 = ((bf16[16,256,128]{2,1,0:T(8,128)(2,1)}), bf16[16,256,128]{2,1,0:T(8,128)(2,1)}, u32[]{:S(2)}, u32[]{:S(2)}) async-start(bf16[16,256,128]{2,1,0:T(8,128)(2,1)} %get-tuple-element.48), calls=%async_computation.4 | async-start | bytes 2097152 | tf_op jit(solution)/shard_map/all_to_all | solution.py:215
  51.2 10.3 %multiply_convert_fusion = bf16[256,4096]{0,1:T(8,128)(2,1)} fusion(bf16[256,4096]{0,1:T(8,128)(2,1)} %copy.50, bf16[2,4096]{0,1:T(8,128)(2,1)} %copy.51, f32[4096]{0:T(1024)S(1)} %bitcast.102, f32[4096]{0:T(1024)S(1)} %bitcast.104, f32[4096]{0:T(1024)S(1)} %bitcast.100, bf16[256,4096]{0,1:T(8,128)(2,1)S(1)} %copy.47, bf16[2,4096]{0,1:T(8,128)(2,1)S(1)} %copy.48, ...), kind=kLoop, calls=%fused_computation.59 | loop fusion | flops 31457280 | bytes 6422528 | tf_op jit(solution)/shard_map/convert_element_type | solution.py:276
  66.8 9.6 %fusion.6 = (bf16[256,4096]{0,1:T(8,128)(2,1)}, f32[256,4096]{0,1:T(8,128)}) fusion(bf16[256,4096]{0,1:T(8,128)(2,1)} %copy.54, bf16[256,4096]{0,1:T(8,128)(2,1)} %copy.44, bf16[2,4096]{0,1:T(8,128)(2,1)} %copy.45, f32[4096]{0:T(1024)S(1)} %bitcast.94, f32[4096]{0:T(1024)S(1)} %bitcast.96, f32[4096]{0:T(1024)S(1)} %bitcast.98), kind=kLoop, calls=%fused_computation.29 | loop fusion | flops 17825792 | bytes 10551296 | tf_op jit(solution)/shard_map/convert_element_type | solution.py:278
  76.4 3.9 copy.55
  84.1 53.4 %all_to_all.40.xg_ref = bf16[16,2,256,128]{3,2,1,0:T(8,128)(2,1)} all-to-all(bf16[16,2,256,128]{3,2,1,0:T(8,128)(2,1)} %get-tuple-element.41), channel_id=1, replica_groups=mesh['ctx'=16,'tp'=2] {'ctx'}, dimensions={0} | all-to-all | bytes 4194304 | tf_op jit(solution)/shard_map/all_to_all | solution.py:215
  137.5 5.3 %all-to-all-start.3 = ((bf16[16,2,256,128]{3,2,1,0:T(8,128)(2,1)}), bf16[16,2,256,128]{3,2,1,0:T(8,128)(2,1)}, u32[]{:S(2)}, u32[]{:S(2)}) async-start(bf16[16,2,256,128]{3,2,1,0:T(8,128)(2,1)} %get-tuple-element.42), calls=%async_computation.3 | async-start | bytes 4194304 | tf_op jit(solution)/shard_map/all_to_all | solution.py:215
  146.8 28.8 %shard_map.163 = (bf16[16,2,256,128]{3,2,1,0:T(8,128)(2,1)}, bf16[16,256,128]{2,1,0:T(8,128)(2,1)}) custom-call(bf16[16,2,256,128]{3,2,1,0:T(8,128)(2,1)} %all_to_all.40.xg_ref, bf16[16,256,128]{2,1,0:T(8,128)(2,1)} %all-to-all-done.1.h_ref, bf16[1024,512]{1,0:T(8,128)(2,1)} %constant.16.clone.first_ref, bf16[512,1024]{1,0:T(8,128)(2,1)} %constant.17.clone.back_ref, ...), custom_call_target="tpu_custom_call" | custom-call | flops 12999999488 | bytes 16000000 | tf_op jit(solution)/shard_map/pallas_call | solution.py:197
  175.6 8.4 %all-to-all-done.3.xg_ref = bf16[16,2,256,128]{3,2,1,0:T(8,128)(2,1)} async-done(((bf16[16,2,256,128]{3,2,1,0:T(8,128)(2,1)}), bf16[16,2,256,128]{3,2,1,0:T(8,128)(2,1)}, u32[]{:S(2)}, u32[]{:S(2)}) %all-to-all-start.3) | async-done | bytes 2097184 | tf_op jit(solution)/shard_map/all_to_all | solution.py:215
  183.9 11.3 %all-to-all-start.2 = ((bf16[16,2,256,128]{3,2,1,0:T(8,128)(2,1)}), bf16[16,2,256,128]{3,2,1,0:T(8,128)(2,1)}, u32[]{:S(2)}, u32[]{:S(2)}) async-start(bf16[16,2,256,128]{3,2,1,0:T(8,128)(2,1)} %get-tuple-element.10), calls=%async_computation.2 | async-start | bytes 4194304 | tf_op jit(solution)/shard_map/all_to_all | solution.py:215
  195.2 28.8 %shard_map.164 = (bf16[16,2,256,128]{3,2,1,0:T(8,128)(2,1)}, bf16[16,256,128]{2,1,0:T(8,128)(2,1)}) custom-call(bf16[16,2,256,128]{3,2,1,0:T(8,128)(2,1)} %all-to-all-done.3.xg_ref, bf16[16,256,128]{2,1,0:T(8,128)(2,1)} %all-to-all-done.4.h_ref, bf16[1024,512]{1,0:T(8,128)(2,1)} %constant.16.clone.first_ref, bf16[512,1024]{1,0:T(8,128)(2,1)} %constant.17.clone.back_ref, ...), custom_call_target="tpu_custom_call" | custom-call | flops 12999999488 | bytes 16000000 | tf_op jit(solution)/shard_map/pallas_call | solution.py:197
  224.1 12.3 %all-to-all-done.2 = bf16[16,2,256,128]{3,2,1,0:T(8,128)(2,1)} async-done(((bf16[16,2,256,128]{3,2,1,0:T(8,128)(2,1)}), bf16[16,2,256,128]{3,2,1,0:T(8,128)(2,1)}, u32[]{:S(2)}, u32[]{:S(2)}) %all-to-all-start.2) | async-done | bytes 2097184 | tf_op jit(solution)/shard_map/all_to_all | solution.py:215
  236.4 11.3 %all-to-all-start.5 = ((bf16[16,2,256,128]{3,2,1,0:T(8,128)(2,1)}), bf16[16,2,256,128]{3,2,1,0:T(8,128)(2,1)}, u32[]{:S(2)}, u32[]{:S(2)}) async-start(bf16[16,2,256,128]{3,2,1,0:T(8,128)(2,1)} %get-tuple-element.11), calls=%async_computation.5 | async-start | bytes 4194304 | tf_op jit(solution)/shard_map/all_to_all | solution.py:215
  250.7 38.1 %all-to-all-done.5 = bf16[16,2,256,128]{3,2,1,0:T(8,128)(2,1)} async-done(((bf16[16,2,256,128]{3,2,1,0:T(8,128)(2,1)}), bf16[16,2,256,128]{3,2,1,0:T(8,128)(2,1)}, u32[]{:S(2)}, u32[]{:S(2)}) %all-to-all-start.5) | async-done | bytes 2097184 | tf_op jit(solution)/shard_map/all_to_all | solution.py:215
  288.8 11.4 %all-to-all-start.6 = ((bf16[16,256,128]{2,1,0:T(8,128)(2,1)}), bf16[16,256,128]{2,1,0:T(8,128)(2,1)}, u32[]{:S(2)}, u32[]{:S(2)}) async-start(bf16[16,256,128]{2,1,0:T(8,128)(2,1)} %get-tuple-element.12), calls=%async_computation.6 | async-start | bytes 2097152 | tf_op jit(solution)/shard_map/all_to_all | solution.py:215
  306.2 5.4 %copy.63 = f32[256,16,2,128]{0,3,2,1:T(8,128)} copy(f32[256,16,2,128]{3,0,1,2:T(8,128)} %get-tuple-element.59) | data formatting | bytes 8388608 | tf_op jit(solution)/shard_map/convert_element_type | solution.py:288
  311.7 11.5 %fusion.24 = (f32[4096]{0:T(1024)S(1)}, f32[4096]{0:T(1024)S(1)}, f32[4096]{0:T(1024)S(1)}, bf16[256,4096]{0,1:T(8,128)(2,1)}) fusion(bf16[256,4096]{0,1:T(8,128)(2,1)} %copy.50, bf16[2,4096]{0,1:T(8,128)(2,1)} %copy.51, bf16[256,4096]{0,1:T(8,128)(2,1)S(1)} %copy.47, bf16[2,4096]{0,1:T(8,128)(2,1)S(1)} %copy.48, f32[4096]{0:T(1024)S(1)} %bitcast.89, ...), kind=kLoop, calls=%fused_computation.47 | loop fusion | flops 33542144 | bytes 10616832 | tf_op jit(solution)/shard_map/reduce_sum | solution.py:50
  323.1 5.3 %copy.59 = f32[256,16,2,128]{0,3,2,1:T(8,128)} copy(f32[256,16,2,128]{3,0,1,2:T(8,128)} %get-tuple-element.60) | data formatting | bytes 8388608 | tf_op jit(solution)/shard_map/convert_element_type | solution.py:287
  333.7 10.7 %fusion.12 = (f32[4096]{0:T(1024)S(1)}, f32[4096]{0:T(1024)S(1)}, f32[4096]{0:T(1024)S(1)}, bf16[256,4096]{0,1:T(8,128)(2,1)}, bf16[256,4096]{0,1:T(8,128)(2,1)}) fusion(bf16[256,4096]{0,1:T(8,128)(2,1)} %copy.44, bf16[2,4096]{0,1:T(8,128)(2,1)} %copy.45, f32[256,16,2,128]{0,3,2,1:T(8,128)} %copy.59, bf16[256,4096]{0,1:T(8,128)(2,1)} %copy.54, ...), kind=kLoop, calls=%fused_computation.35 | loop fusion | flops 22007808 | bytes 16842752 | tf_op jit(solution)/shard_map/reduce_sum | solution.py:50
  345.9 6.9 %all-to-all-start.7 = ((bf16[16,256,128]{2,1,0:T(8,128)(2,1)}), bf16[16,256,128]{2,1,0:T(8,128)(2,1)}, u32[]{:S(2)}, u32[]{:S(2)}) async-start(bf16[16,256,128]{2,1,0:T(8,128)(2,1)} %get-tuple-element.13), calls=%async_computation.7 | async-start | bytes 2097152 | tf_op jit(solution)/shard_map/all_to_all | solution.py:215
  352.9 18.0 %fusion.18 = (f32[4096]{0:T(1024)S(1)}, f32[4096]{0:T(1024)S(1)}, f32[4096]{0:T(1024)S(1)}, bf16[256,4096]{0,1:T(8,128)(2,1)}, bf16[256,4096]{0,1:T(8,128)(2,1)}) fusion(bf16[256,4096]{0,1:T(8,128)(2,1)S(1)} %copy.47, bf16[2,4096]{0,1:T(8,128)(2,1)S(1)} %copy.48, bf16[256,4096]{0,1:T(8,128)(2,1)} %copy.50, bf16[2,4096]{0,1:T(8,128)(2,1)} %copy.51, ...), kind=kLoop, calls=%fused_computation.41 | loop fusion | flops 49270784 | bytes 14827520 | tf_op jit(solution)/shard_map/reduce_sum | solution.py:50
  381.3 4.1 copy.73
  385.3 4.2 copy.69
  399.4 6.3 %fusion.10 = bf16[256,4096]{0,1:T(8,128)(2,1)} fusion(bf16[256,4096]{0,1:T(8,128)(2,1)S(1)} %copy-done.1, bf16[2,4096]{0,1:T(8,128)(2,1)S(1)} %copy.61, f32[4096]{0:T(1024)} %bitcast.95, f32[4096]{0:T(1024)} %bitcast.97, f32[4096]{0:T(1024)} %bitcast.99), kind=kLoop, calls=%fused_computation.33 | loop fusion | flops 15728640 | bytes 4259840 | tf_op jit(solution)/shard_map/convert_element_type | solution.py:298
  405.8 4.2 copy.72
  410.0 4.1 copy.70
  418.8 5.4 %fusion.16 = bf16[256,4096]{0,1:T(8,128)(2,1)} fusion(bf16[256,4096]{0,1:T(8,128)(2,1)S(1)} %copy-done.2, bf16[2,4096]{0,1:T(8,128)(2,1)S(1)} %copy.65, f32[4096]{0:T(1024)S(1)} %bitcast.90, f32[4096]{0:T(1024)S(1)} %bitcast.93, f32[4096]{0:T(1024)S(1)} %bitcast.87), kind=kLoop, calls=%fused_computation.39 | loop fusion | flops 15728640 | bytes 4259840 | tf_op jit(solution)/shard_map/convert_element_type | solution.py:299
  424.2 4.1 copy.71
  (90 shorter events, 76.6 us)
Async XLA Ops:
  7.7 20.1 %copy-start.12 = (f32[3,3,4096]{2,1,0:T(4,128)S(1)}, f32[3,3,4096]{2,1,0:T(4,128)}, u32[]{:S(2)}) copy-start(f32[3,3,4096]{2,1,0:T(4,128)} %param.16) | copy-start | bytes 442372
  9.3 36.1 %all-to-all-start.1 = ((bf16[16,256,128]{2,1,0:T(8,128)(2,1)}), bf16[16,256,128]{2,1,0:T(8,128)(2,1)}, u32[]{:S(2)}, u32[]{:S(2)}) async-start(bf16[16,256,128]{2,1,0:T(8,128)(2,1)} %get-tuple-element.47), calls=%async_computation.1 | async-start | bytes 2097152 | tf_op jit(solution)/shard_map/all_to_all | solution.py:215
  17.6 25.9 %collective-permute-start.1 = (bf16[2,4096]{1,0:T(2,128)(2,1)S(1)}, bf16[2,4096]{1,0:T(2,128)(2,1)S(1)}, u32[]{:S(2)}, u32[]{:S(2)}) collective-permute-start(bf16[2,4096]{1,0:T(2,128)(2,1)S(1)} %slice.152), channel_id=1, source_target_pairs={{0,2},{2,4},{4,6},{6,8},{8,10},{10,12},{12,14},{14,16},{16,18},{18... | collective-permute-start | bytes 49160 | tf_op jit(solution)/shard_map/ppermute | solution.py:20
  21.4 22.6 %collective-permute-start.2 = (bf16[2,4096]{1,0:T(2,128)(2,1)}, bf16[2,4096]{1,0:T(2,128)(2,1)S(1)}, u32[]{:S(2)}, u32[]{:S(2)}) collective-permute-start(bf16[2,4096]{1,0:T(2,128)(2,1)} %slice.158), channel_id=1, source_target_pairs={{0,2},{2,4},{4,6},{6,8},{8,10},{10,12},{12,14},{14,16},{16,18},{18... | collective-permute-start | bytes 49160 | tf_op jit(solution)/shard_map/ppermute | solution.py:20
  25.8 39.6 %collective-permute-start = (bf16[2,4096]{1,0:T(2,128)(2,1)S(1)}, bf16[2,4096]{1,0:T(2,128)(2,1)S(1)}, u32[]{:S(2)}, u32[]{:S(2)}) collective-permute-start(bf16[2,4096]{1,0:T(2,128)(2,1)S(1)} %slice.146), channel_id=1, source_target_pairs={{0,2},{2,4},{4,6},{6,8},{8,10},{10,12},{12,14},{14,16},{16,18},{18... | collective-permute-start | bytes 49160 | tf_op jit(solution)/shard_map/ppermute | solution.py:20
  28.0 38.8 %copy-start.9 = (f32[1,1,4096]{2,1,0:T(1,128)}, f32[1,1,4096]{2,1,0:T(1,128)S(1)}, u32[]{:S(2)}) copy-start(f32[1,1,4096]{2,1,0:T(1,128)S(1)} %get-tuple-element.53) | copy-start | bytes 49156
  28.0 38.8 %copy-start.10 = (f32[1,1,4096]{2,1,0:T(1,128)}, f32[1,1,4096]{2,1,0:T(1,128)S(1)}, u32[]{:S(2)}) copy-start(f32[1,1,4096]{2,1,0:T(1,128)S(1)} %get-tuple-element.54) | copy-start | bytes 49156
  28.0 38.8 %copy-start.11 = (f32[1,1,4096]{2,1,0:T(1,128)}, f32[1,1,4096]{2,1,0:T(1,128)S(1)}, u32[]{:S(2)}) copy-start(f32[1,1,4096]{2,1,0:T(1,128)S(1)} %get-tuple-element.55) | copy-start | bytes 49156
  28.0 283.7 %copy-start.5 = (f32[1,1,4096]{2,1,0:T(1,128)}, f32[1,1,4096]{2,1,0:T(1,128)S(1)}, u32[]{:S(2)}) copy-start(f32[1,1,4096]{2,1,0:T(1,128)S(1)} %get-tuple-element.51) | copy-start | bytes 49156
  28.0 283.7 %copy-start.7 = (f32[1,1,4096]{2,1,0:T(1,128)}, f32[1,1,4096]{2,1,0:T(1,128)S(1)}, u32[]{:S(2)}) copy-start(f32[1,1,4096]{2,1,0:T(1,128)S(1)} %get-tuple-element.52) | copy-start | bytes 49156
  45.4 38.7 %all-to-all-start.4 = ((bf16[16,256,128]{2,1,0:T(8,128)(2,1)}), bf16[16,256,128]{2,1,0:T(8,128)(2,1)}, u32[]{:S(2)}, u32[]{:S(2)}) async-start(bf16[16,256,128]{2,1,0:T(8,128)(2,1)} %get-tuple-element.48), calls=%async_computation.4 | async-start | bytes 2097152 | tf_op jit(solution)/shard_map/all_to_all | solution.py:215
  84.1 58.7 %copy-start.13 = (f32[33,128]{1,0:T(8,128)S(1)}, f32[33,128]{1,0:T(8,128)}, u32[]{:S(2)}) copy-start(f32[33,128]{1,0:T(8,128)} %constant.20.clone) | copy-start | bytes 50692
  137.5 7.3 %copy-start.14 = (f32[33,128]{1,0:T(8,128)S(1)}, f32[33,128]{1,0:T(8,128)}, u32[]{:S(2)}) copy-start(f32[33,128]{1,0:T(8,128)} %constant.21.clone) | copy-start | bytes 50692
  137.5 46.5 %all-to-all-start.3 = ((bf16[16,2,256,128]{3,2,1,0:T(8,128)(2,1)}), bf16[16,2,256,128]{3,2,1,0:T(8,128)(2,1)}, u32[]{:S(2)}, u32[]{:S(2)}) async-start(bf16[16,2,256,128]{3,2,1,0:T(8,128)(2,1)} %get-tuple-element.42), calls=%async_computation.3 | async-start | bytes 4194304 | tf_op jit(solution)/shard_map/all_to_all | solution.py:215
  183.9 52.4 %all-to-all-start.2 = ((bf16[16,2,256,128]{3,2,1,0:T(8,128)(2,1)}), bf16[16,2,256,128]{3,2,1,0:T(8,128)(2,1)}, u32[]{:S(2)}, u32[]{:S(2)}) async-start(bf16[16,2,256,128]{3,2,1,0:T(8,128)(2,1)} %get-tuple-element.10), calls=%async_computation.2 | async-start | bytes 4194304 | tf_op jit(solution)/shard_map/all_to_all | solution.py:215
  236.4 52.4 %all-to-all-start.5 = ((bf16[16,2,256,128]{3,2,1,0:T(8,128)(2,1)}), bf16[16,2,256,128]{3,2,1,0:T(8,128)(2,1)}, u32[]{:S(2)}, u32[]{:S(2)}) async-start(bf16[16,2,256,128]{3,2,1,0:T(8,128)(2,1)} %get-tuple-element.11), calls=%async_computation.5 | async-start | bytes 4194304 | tf_op jit(solution)/shard_map/all_to_all | solution.py:215
  288.8 57.1 %all-to-all-start.6 = ((bf16[16,256,128]{2,1,0:T(8,128)(2,1)}), bf16[16,256,128]{2,1,0:T(8,128)(2,1)}, u32[]{:S(2)}, u32[]{:S(2)}) async-start(bf16[16,256,128]{2,1,0:T(8,128)(2,1)} %get-tuple-element.12), calls=%async_computation.6 | async-start | bytes 2097152 | tf_op jit(solution)/shard_map/all_to_all | solution.py:215
  300.3 1.9 copy-start.3
  300.3 2.2 copy-start.4
  332.4 12.1 %collective-permute-start.5 = (bf16[2,4096]{1,0:T(2,128)(2,1)S(1)}, bf16[2,4096]{1,0:T(2,128)(2,1)S(1)}, u32[]{:S(2)}, u32[]{:S(2)}) collective-permute-start(bf16[2,4096]{1,0:T(2,128)(2,1)S(1)} %copy.66), channel_id=1, source_target_pairs={{2,0},{4,2},{6,4},{8,6},{10,8},{12,10},{14,12},{16,14},{18,16},{20... | collective-permute-start | bytes 49160 | tf_op jit(solution)/shard_map/ppermute | solution.py:20
  345.9 31.0 %all-to-all-start.7 = ((bf16[16,256,128]{2,1,0:T(8,128)(2,1)}), bf16[16,256,128]{2,1,0:T(8,128)(2,1)}, u32[]{:S(2)}, u32[]{:S(2)}) async-start(bf16[16,256,128]{2,1,0:T(8,128)(2,1)} %get-tuple-element.13), calls=%async_computation.7 | async-start | bytes 2097152 | tf_op jit(solution)/shard_map/all_to_all | solution.py:215
  352.8 18.6 %copy-start = (bf16[256,4096]{0,1:T(8,128)(2,1)S(1)}, bf16[256,4096]{0,1:T(8,128)(2,1)}, u32[]{:S(2)}) copy-start(bf16[256,4096]{0,1:T(8,128)(2,1)} %get-tuple-element.35) | copy-start | bytes 6291460
  371.0 2.8 collective-permute-start.6
  372.5 20.9 %collective-permute-start.3 = (bf16[2,4096]{1,0:T(2,128)(2,1)}, bf16[2,4096]{1,0:T(2,128)(2,1)}, u32[]{:S(2)}, u32[]{:S(2)}) collective-permute-start(bf16[2,4096]{1,0:T(2,128)(2,1)} %copy.60), channel_id=1, source_target_pairs={{2,0},{4,2},{6,4},{8,6},{10,8},{12,10},{14,12},{16,14},{18,16},{20... | collective-permute-start | bytes 49160 | tf_op jit(solution)/shard_map/ppermute | solution.py:20
  374.5 20.1 %collective-permute-start.7 = (f32[3,3,4096]{2,1,0:T(4,128)}, f32[3,3,4096]{2,1,0:T(4,128)}, u32[]{:S(2)}, u32[]{:S(2)}) collective-permute-start(f32[3,3,4096]{2,1,0:T(4,128)} %fusion.38), channel_id=1, source_target_pairs={{0,4},{2,6},{4,0},{6,2},{8,12},{10,14},{12,8},{14,10},{16,20},{18,... | collective-permute-start | bytes 442376 | tf_op jit(solution)/shard_map/ppermute | solution.py:222
  385.3 14.1 %copy-start.1 = (bf16[256,4096]{0,1:T(8,128)(2,1)S(1)}, bf16[256,4096]{0,1:T(8,128)(2,1)}, u32[]{:S(2)}) copy-start(bf16[256,4096]{0,1:T(8,128)(2,1)} %get-tuple-element.35) | copy-start | bytes 6291460
  391.8 22.2 %collective-permute-start.4 = (bf16[2,4096]{1,0:T(2,128)(2,1)}, bf16[2,4096]{1,0:T(2,128)(2,1)}, u32[]{:S(2)}, u32[]{:S(2)}) collective-permute-start(bf16[2,4096]{1,0:T(2,128)(2,1)} %copy.64), channel_id=1, source_target_pairs={{2,0},{4,2},{6,4},{8,6},{10,8},{12,10},{14,12},{16,14},{18,16},{20... | collective-permute-start | bytes 49160 | tf_op jit(solution)/shard_map/ppermute | solution.py:20
  396.3 19.0 %collective-permute-start.8 = (f32[3,3,4096]{2,1,0:T(4,128)}, f32[3,3,4096]{2,1,0:T(4,128)}, u32[]{:S(2)}, u32[]{:S(2)}) collective-permute-start(f32[3,3,4096]{2,1,0:T(4,128)} %fusion.44), channel_id=1, source_target_pairs={{0,8},{2,10},{4,12},{6,14},{8,0},{10,2},{12,4},{14,6},{16,24},{18,... | collective-permute-start | bytes 442376 | tf_op jit(solution)/shard_map/ppermute | solution.py:222
  405.8 13.0 %copy-start.2 = (bf16[256,4096]{0,1:T(8,128)(2,1)S(1)}, bf16[256,4096]{0,1:T(8,128)(2,1)}, u32[]{:S(2)}) copy-start(bf16[256,4096]{0,1:T(8,128)(2,1)} %get-tuple-element.36) | copy-start | bytes 6291460
  405.8 13.0 %copy-start.6 = (f32[1,1,4096]{2,1,0:T(1,128)S(1)}, f32[1,1,4096]{2,1,0:T(1,128)}, u32[]{:S(2)}) copy-start(f32[1,1,4096]{2,1,0:T(1,128)} %copy-done.5) | copy-start | bytes 49156
  405.8 13.0 %copy-start.8 = (f32[1,1,4096]{2,1,0:T(1,128)S(1)}, f32[1,1,4096]{2,1,0:T(1,128)}, u32[]{:S(2)}) copy-start(f32[1,1,4096]{2,1,0:T(1,128)} %copy-done.7) | copy-start | bytes 49156
  416.4 12.2 %collective-permute-start.9 = (f32[3,3,4096]{2,1,0:T(4,128)S(1)}, f32[3,3,4096]{2,1,0:T(4,128)}, u32[]{:S(2)}, u32[]{:S(2)}) collective-permute-start(f32[3,3,4096]{2,1,0:T(4,128)S(1)} %add.62), channel_id=1, source_target_pairs={{0,16},{2,18},{4,20},{6,22},{8,24},{10,26},{12,28},{14,30},{16,0},... | collective-permute-start | bytes 442376 | tf_op jit(solution)/shard_map/ppermute | solution.py:222

commit v2 on v1

--- a/solution.py
+++ b/solution.py
@@ -18,41 +18,6 @@
     count = lax.axis_size(axis)
     pairs = [(i, i + by) for i in range(count) if 0 <= i + by < count]
     return lax.ppermute(x, axis, pairs)
-
-
-def short_filter(extended, weights, local_rows):
-    tap_count = weights.shape[0]
-    result = jnp.zeros((local_rows, extended.shape[1]), jnp.float32)
-    for lag_index in range(tap_count):
-        offset_row = tap_count - 1 - lag_index
-        result = result + weights[lag_index] * extended[
-            offset_row : offset_row + local_rows
-        ].astype(jnp.float32)
-    return result
-
-
-def filter_back(extended, weights, local_rows):
-    tap_count = weights.shape[0]
-    result = jnp.zeros((local_rows, extended.shape[1]), jnp.float32)
-    for lag_index in range(tap_count):
-        result = result + weights[lag_index] * extended[lag_index : lag_index + local_rows].astype(
-            jnp.float32
-        )
-    return result
-
-
-def weight_terms(grads, extended, tap_count, local_rows):
-    grad_float = grads.astype(jnp.float32)
-    terms = []
-    for lag_index in range(tap_count):
-        offset_row = tap_count - 1 - lag_index
-        terms.append(
-            jnp.sum(
-                grad_float * extended[offset_row : offset_row + local_rows].astype(jnp.float32),
-                axis=0,
-            )
-        )
-    return jnp.stack(terms)
 
 
 def grid_tables(outer_len):
@@ -80,6 +45,7 @@
 def spectral_kernel(
     inv_root,
     scale,
+    chunk,
     xg_ref,
     h_ref,
     first_ref,
@@ -94,7 +60,7 @@
 ):
     k_count = work.shape[0]
     half_rows = k_count - 1
-    rows_per = h_ref.shape[1] // S
+    rows_per = h_ref.shape[2] // S
 
     def first_section(step, carry):
         at = pl.multiple_of(step * G, G)
@@ -106,7 +72,7 @@
                     [
                         xg_ref[r // rows_per, 0, rows, :],
                         xg_ref[r // rows_per, 1, rows, :],
-                        h_ref[r // rows_per, rows, :],
+                        h_ref[r // rows_per, chunk, rows, :],
                     ],
                     axis=1,
                 )
@@ -188,17 +154,17 @@
     lax.fori_loop(0, S // G, last_section, 0)
 
 
-def transform_chunk(xg, h, tables, inv_root, scale):
+def transform_chunk(xg, h, chunk, tables, inv_root, scale):
     k_count = tables[4].shape[0]
     lanes = h.shape[-1]
     if lanes < LANES:
         xg = jnp.pad(xg, ((0, 0),) * 3 + ((0, LANES - lanes),))
-        h = jnp.pad(h, ((0, 0),) * 2 + ((0, LANES - lanes),))
+        h = jnp.pad(h, ((0, 0),) * 3 + ((0, LANES - lanes),))
     cg, gf = pl.pallas_call(
-        functools.partial(spectral_kernel, inv_root, scale),
+        functools.partial(spectral_kernel, inv_root, scale, chunk),
         out_shape=(
             jax.ShapeDtypeStruct(xg.shape, jnp.bfloat16),
-            jax.ShapeDtypeStruct(h.shape, jnp.bfloat16),
+            jax.ShapeDtypeStruct((h.shape[0],) + h.shape[2:], jnp.bfloat16),
         ),
         in_specs=[pl.BlockSpec(memory_space=pltpu.VMEM)] * 8,
         out_specs=(pl.BlockSpec(memory_space=pltpu.VMEM),) * 2,
@@ -209,6 +175,114 @@
         ),
     )(xg, h, *tables)
     return cg[..., :lanes], gf[..., :lanes]
+
+
+def later(x, head):
+    row = lax.broadcasted_iota(jnp.int32, x.shape, 0)
+    one = jnp.where(row == 0, head[1:2], pltpu.roll(x, 1, 0))
+    two = jnp.where(row == 0, head[0:1], jnp.where(row == 1, head[1:2], pltpu.roll(x, 2, 0)))
+    return (x, one, two)
+
+
+def sooner(x, tail):
+    count = x.shape[0]
+    row = lax.broadcasted_iota(jnp.int32, x.shape, 0)
+    one = jnp.where(row == count - 1, tail[0:1], pltpu.roll(x, count - 1, 0))
+    two = jnp.where(
+        row == count - 1,
+        tail[1:2],
+        jnp.where(row == count - 2, tail[0:1], pltpu.roll(x, count - 2, 0)),
+    )
+    return (x, one, two)
+
+
+def weigh(shifted, weights):
+    return sum(weights[j : j + 1] * shifted[j] for j in range(len(shifted)))
+
+
+def as_float(ref):
+    return ref[...].astype(jnp.float32)
+
+
+def rounded(x):
+    return x.astype(jnp.bfloat16)
+
+
+def filter_kernel(h_ref, out_ref):
+    per, chunks, _, lanes = out_ref.shape
+    for i in range(per):
+        for c in range(chunks):
+            at = (i * chunks + c) * lanes
+            out_ref[i, c] = h_ref[:, at : at + lanes]
+
+
+def unpack_kernel(gf_ref, out_ref):
+    per, chunks, _, lanes = gf_ref.shape
+    for i in range(per):
+        for c in range(chunks):
+            at = (i * chunks + c) * lanes
+            out_ref[:, at : at + lanes] = gf_ref[i, c]
+
+
+def entry_kernel(q_ref, k_ref, v_ref, cot_ref, ahead_ref, w_ref, *outs):
+    ahead = as_float(ahead_ref)
+    per, _, _, lanes = outs[0].shape
+    shorts = []
+    for i, ref in enumerate((q_ref, k_ref, v_ref)):
+        shorts.append(weigh(later(as_float(ref), ahead[2 * i : 2 * i + 2]), w_ref[i]))
+    mixed = rounded(shorts[1] * shorts[2])
+    grad_conv = rounded(as_float(cot_ref) * shorts[0])
+    for i in range(per):
+        for c, out in enumerate(outs):
+            at = (i * len(outs) + c) * lanes
+            out[i, 0] = mixed[:, at : at + lanes]
+            out[i, 1] = grad_conv[:, at : at + lanes]
+
+
+def local_grads(q_ref, k_ref, v_ref, cot_ref, ahead_ref, w_ref, conv, grad_mixed):
+    ahead = as_float(ahead_ref)
+    shifted = []
+    shorts = []
+    for i, ref in enumerate((q_ref, k_ref, v_ref)):
+        shifted.append(later(as_float(ref), ahead[2 * i : 2 * i + 2]))
+        shorts.append(weigh(shifted[i], w_ref[i]))
+    grads = [as_float(cot_ref) * conv, grad_mixed * shorts[2], grad_mixed * shorts[1]]
+    grads = [rounded(g).astype(jnp.float32) for g in grads]
+    return shifted, shorts, grads
+
+
+def gather_lanes(cg_refs, which, blocks):
+    parts = [cg[i, which] for i in blocks for cg in cg_refs]
+    return jnp.concatenate(parts, axis=1).astype(jnp.float32)
+
+
+def edge_kernel(q_ref, k_ref, v_ref, cot_ref, ahead_ref, w_ref, *rest):
+    cg_refs, edge_ref = rest[:-1], rest[-1]
+    blocks = range(cg_refs[0].shape[0])
+    conv = gather_lanes(cg_refs, 0, blocks)
+    grad_mixed = gather_lanes(cg_refs, 1, blocks)
+    _, _, grads = local_grads(
+        q_ref, k_ref, v_ref, cot_ref, ahead_ref, w_ref, conv, grad_mixed
+    )
+    for i in range(3):
+        edge_ref[2 * i : 2 * i + 2, :] = rounded(grads[i][:2])
+
+
+def exit_kernel(chunks, q_ref, k_ref, v_ref, cot_ref, ahead_ref, w_ref, behind_ref, *rest):
+    cg_refs = rest[:chunks]
+    out_ref, gq_ref, gk_ref, gv_ref, short_ref = rest[chunks:]
+    blocks = range(cg_refs[0].shape[0])
+    conv = gather_lanes(cg_refs, 0, blocks)
+    grad_mixed = gather_lanes(cg_refs, 1, blocks)
+    shifted, shorts, grads = local_grads(
+        q_ref, k_ref, v_ref, cot_ref, ahead_ref, w_ref, conv, grad_mixed
+    )
+    out_ref[...] = rounded(shorts[0] * conv)
+    behind = as_float(behind_ref)
+    for i, ref in enumerate((gq_ref, gk_ref, gv_ref)):
+        ref[...] = rounded(weigh(sooner(grads[i], behind[2 * i : 2 * i + 2]), w_ref[i]))
+        for j in range(3):
+            short_ref[i, j : j + 1, :] = jnp.sum(grads[i] * shifted[i][j], axis=0, keepdims=True)
 
 
 def exchange(x):
@@ -236,12 +310,16 @@
     own = channels // ctx_size
     lanes = min(own, LANES)
     chunks = own // lanes
-
-    def to_owners(x):
-        return x.reshape(local_rows, ctx_size, chunks, lanes).transpose(2, 1, 0, 3)
-
-    def from_owners(parts):
-        return jnp.stack(parts).transpose(2, 1, 0, 3).reshape(local_rows, channels)
+    width = max(own, LANES)
+    per = width // own
+    steps = channels // width
+    limit = pltpu.CompilerParams(vmem_limit_bytes=58 * 1024 * 1024)
+    stream = pl.BlockSpec((local_rows, width), lambda i: (0, i))
+    rim = pl.BlockSpec((3 * rim_rows, width), lambda i: (0, i))
+    taps = pl.BlockSpec((3, tap_count, width), lambda i: (0, 0, i))
+    pair = pl.BlockSpec((per, 2, local_rows, lanes), lambda i: (i, 0, 0, 0))
+    packed = pl.BlockSpec((per, chunks, local_rows, lanes), lambda i: (i, 0, 0, 0))
+    whole = jax.ShapeDtypeStruct((local_rows, channels), jnp.bfloat16)
 
     first, back, inner_fwd, inner_back, turn_cos, turn_sin = grid_tables(outer_len)
     tables = (
@@ -256,56 +334,75 @@
             jnp.asarray(turn_sin, jnp.float32)[:, :, None], turn_sin.shape + (LANES,)
         ),
     )
-    filter_parts = to_owners(long_filter)
-    h_parts = [exchange(filter_parts[c]) for c in range(chunks)]
-    ahead = from_behind(
-        (
-            query_in[local_rows - rim_rows :],
-            key_in[local_rows - rim_rows :],
-            value_in[local_rows - rim_rows :],
-        ),
-        "ctx",
-        1,
-    )
-    ext_query = jnp.concatenate([ahead[0], query_in], axis=0)
-    ext_key = jnp.concatenate([ahead[1], key_in], axis=0)
-    ext_value = jnp.concatenate([ahead[2], value_in], axis=0)
-    q_short = short_filter(ext_query, short_weight[0], local_rows)
-    k_short = short_filter(ext_key, short_weight[1], local_rows)
-    v_short = short_filter(ext_value, short_weight[2], local_rows)
-    mixed = (k_short * v_short).astype(jnp.bfloat16)
-    cot_float = cotangent.astype(jnp.float32)
-    grad_conv = (cot_float * q_short).astype(jnp.bfloat16)
-    xg_parts = jnp.stack([to_owners(mixed), to_owners(grad_conv)], axis=2)
-    xg_parts = [exchange(xg_parts[c]) for c in range(chunks)]
+    tails = jnp.concatenate([x[local_rows - rim_rows :] for x in (query_in, key_in, value_in)])
+    ahead = from_behind(tails, "ctx", 1)
+    h = exchange(
+        pl.pallas_call(
+            filter_kernel,
+            grid=(steps,),
+            out_shape=jax.ShapeDtypeStruct((ctx_size, chunks, local_rows, lanes), jnp.bfloat16),
+            in_specs=[stream],
+            out_specs=packed,
+            compiler_params=limit,
+        )(long_filter)
+    )
+    streams = (query_in, key_in, value_in, cotangent, ahead, short_weight)
+    xg_parts = pl.pallas_call(
+        entry_kernel,
+        grid=(steps,),
+        out_shape=(
+            jax.ShapeDtypeStruct((ctx_size, 2, local_rows, lanes), jnp.bfloat16),
+        )
+        * chunks,
+        in_specs=[stream] * 4 + [rim, taps],
+        out_specs=(pair,) * chunks,
+        compiler_params=limit,
+        cost_estimate=pl.CostEstimate(
+            flops=100_000_000, bytes_accessed=12_000_000, transcendentals=0
+        ),
+    )(*streams)
+    xg_parts = [exchange(xg) for xg in xg_parts]
     cg_parts, gf_parts = [], []
-    for xg, h in zip(xg_parts, h_parts):
-        cg, gf = transform_chunk(xg, h, tables, inv_root, 1.0 / fft_size)
+    for c, xg in enumerate(xg_parts):
+        cg, gf = transform_chunk(xg, h, c, tables, inv_root, 1.0 / fft_size)
         cg_parts.append(exchange(cg))
         gf_parts.append(gf)
-    gf_parts = [exchange(gf) for gf in gf_parts]
-    conv = from_owners([part[:, 0] for part in cg_parts]).astype(jnp.float32)
-    grad_mixed = from_owners([part[:, 1] for part in cg_parts]).astype(jnp.float32)
-    grad_filter = from_owners(gf_parts)
-    block_out = (q_short * conv).astype(jnp.bfloat16)
-    gq_short = (cot_float * conv).astype(jnp.bfloat16)
-    gk_short = (grad_mixed * v_short).astype(jnp.bfloat16)
-    gv_short = (grad_mixed * k_short).astype(jnp.bfloat16)
-    behind = from_behind((gq_short[:rim_rows], gk_short[:rim_rows], gv_short[:rim_rows]), "ctx", -1)
-    ext_gq = jnp.concatenate([gq_short, behind[0]], axis=0)
-    ext_gk = jnp.concatenate([gk_short, behind[1]], axis=0)
-    ext_gv = jnp.concatenate([gv_short, behind[2]], axis=0)
-    grad_query = filter_back(ext_gq, short_weight[0], local_rows).astype(jnp.bfloat16)
-    grad_key = filter_back(ext_gk, short_weight[1], local_rows).astype(jnp.bfloat16)
-    grad_value = filter_back(ext_gv, short_weight[2], local_rows).astype(jnp.bfloat16)
-    short_part = jnp.stack(
-        [
-            weight_terms(gq_short, ext_query, tap_count, local_rows),
-            weight_terms(gk_short, ext_key, tap_count, local_rows),
-            weight_terms(gv_short, ext_value, tap_count, local_rows),
+    gf_back = exchange(jnp.stack(gf_parts, axis=1))
+    top = pl.BlockSpec((G, channels), lambda i: (0, 0))
+    edge = pl.pallas_call(
+        edge_kernel,
+        grid=(1,),
+        out_shape=jax.ShapeDtypeStruct((3 * rim_rows, channels), jnp.bfloat16),
+        in_specs=[top] * 4
+        + [
+            pl.BlockSpec((3 * rim_rows, channels), lambda i: (0, 0)),
+            pl.BlockSpec((3, tap_count, channels), lambda i: (0, 0, 0)),
         ]
-    )
+        + [pl.BlockSpec((ctx_size, 2, G, lanes), lambda i: (0, 0, 0, 0))] * chunks,
+        out_specs=pl.BlockSpec((3 * rim_rows, channels), lambda i: (0, 0)),
+        compiler_params=limit,
+    )(*streams, *cg_parts)
+    behind = from_behind(edge, "ctx", -1)
+    block_out, grad_query, grad_key, grad_value, short_part = pl.pallas_call(
+        functools.partial(exit_kernel, chunks),
+        grid=(steps,),
+        out_shape=(whole,) * 4 + (jax.ShapeDtypeStruct((3, tap_count, channels), jnp.float32),),
+        in_specs=[stream] * 4 + [rim, taps, rim] + [pair] * chunks,
+        out_specs=(stream,) * 4 + (taps,),
+        compiler_params=limit,
+        cost_estimate=pl.CostEstimate(
+            flops=200_000_000, bytes_accessed=20_000_000, transcendentals=0
+        ),
+    )(*streams, behind, *cg_parts)
     grad_short = sum_over(short_part, "ctx") * inv_root
+    grad_filter = pl.pallas_call(
+        unpack_kernel,
+        grid=(steps,),
+        out_shape=whole,
+        in_specs=[packed],
+        out_specs=stream,
+        compiler_params=limit,
+    )(gf_back)
     return (block_out, grad_query, grad_key, grad_value, grad_short, grad_filter)
 
 

time: 433 us -> 395 us (0.912)
  other arithmetic: 86.5 us -> 4.63 us
  local copies, waits for them, and re-layouts: 93 us -> 11.8 us
  Pallas kernels: 57.6 us -> 111 us
  waiting for transfers between devices: 59 us -> 94.9 us
  blocking collectives: 53.4 us -> 72.3 us
  starting transfers between devices: 79.7 us -> 97.3 us
    pallas_call x2 -> x7, Pallas kernels: 57.6 us -> 111 us  [the longest x2 58.1 us: transform_chunk(): pl.pallas_call(functools.partial(spectral_kernel, inv_root, scale, chunk)...]
    reduce_sum x3 -> x0, other arithmetic: 40.2 us -> none  [weight_terms(): jnp.sum(grad_float * extended[offset_row:offset_row + local_rows].astype(...]
    ppermute x4, starting transfers between devices: 8.43 us -> 47.4 us  [sum_over(): x = x + lax.ppermute(x, axis, [(i, i ^ step) for i in range(count)])]
    convert_element_type x5 -> x0, other arithmetic: 35.4 us -> none  [the longest x1 10.3 us: on_device(): mixed = (k_short * v_short).astype(jnp.bfloat16)]
    unnamed x40 -> x18, local copies, waits for them, and re-layouts: 40.6 us -> 5.25 us
    all_to_all x7 -> x5, waiting for transfers between devices: 58.8 us -> 80.4 us  [exchange(): return lax.all_to_all(x, 'ctx', split_axis=0, concat_axis=0, tiled=True)]
    all_to_all x1, blocking collectives: 53.4 us -> 72.3 us  [exchange(): return lax.all_to_all(x, 'ctx', split_axis=0, concat_axis=0, tiled=True)]
    all_to_all x7 -> x5, starting transfers between devices: 59.4 us -> 46.3 us  [exchange(): return lax.all_to_all(x, 'ctx', split_axis=0, concat_axis=0, tiled=True)]
  transfers between devices with their start and end apart: 17 -> 11, of which waited for: 4 -> 9; matrix products, arithmetic and copies ran while one was open for 39% -> 3% of each run, Pallas kernels for 13% -> 26%
where the time goes in v2:
time: 395 us; the launch traced here: 393 us
  Pallas kernels  111 us (28%)
  starting transfers between devices  97.3 us (25%)
  waiting for transfers between devices  94.9 us (24%)
  blocking collectives  72.3 us (18%)
  local copies, waits for them, and re-layouts  11.8 us (3%)
  other arithmetic  4.63 us (1%)
    all_to_all x5, waiting for transfers between devices, exchange(): return lax.all_to_all(x, 'ctx', split_axis=0, concat_axis=0, tiled=True)  80.4 us
    all_to_all x1, blocking collectives, exchange(): return lax.all_to_all(x, 'ctx', split_axis=0, concat_axis=0, tiled=True)  72.3 us
    pallas_call x2, Pallas kernels, transform_chunk(): pl.pallas_call(functools.partial(spectral_kernel, inv_root, scale, chunk)...  58.1 us
    ppermute x4, starting transfers between devices, sum_over(): x = x + lax.ppermute(x, axis, [(i, i ^ step) for i in range(count)])  47.4 us
    all_to_all x5, starting transfers between devices, exchange(): return lax.all_to_all(x, 'ctx', split_axis=0, concat_axis=0, tiled=True)  46.3 us
    pallas_call x1, Pallas kernels, on_device(): pl.pallas_call(functools.partial(exit_kernel, chunks), grid=(steps,), out...  18.8 us
    pallas_call x1, Pallas kernels, on_device(): pl.pallas_call(entry_kernel, grid=(steps,), out_shape=(jax.ShapeDtypeStru...  12.8 us
    ppermute x4, waiting for transfers between devices, sum_over(): x = x + lax.ppermute(x, axis, [(i, i ^ step) for i in range(count)])  11.6 us
  transfers between devices with their start and end apart: 11, of which 9 were waited for; matrix products, arithmetic and copies ran while one was open for 3% of the time, Pallas kernels for 26%

profile of v2, /device:TPU:0, one launch (start us, length us, event | category | flops | bytes accessed | tf_op | source)
XLA Modules:
  0.0 392.6 jit_solution(15164893021694137730)
XLA Ops:
  0.6 9.6 %shard_map.164 = bf16[16,2,256,128]{3,2,1,0:T(8,128)(2,1)} custom-call(bf16[256,4096]{1,0:T(8,128)(2,1)} %h_ref.1), custom_call_target="tpu_custom_call" | custom-call | tf_op jit(solution)/shard_map/pallas_call | solution.py:340
  10.2 7.4 %all-to-all-start.1 = ((bf16[16,2,256,128]{3,2,1,0:T(8,128)(2,1)}), bf16[16,2,256,128]{3,2,1,0:T(8,128)(2,1)S(1)}, u32[]{:S(2)}, u32[]{:S(2)}) async-start(bf16[16,2,256,128]{3,2,1,0:T(8,128)(2,1)} %shard_map.164), calls=%async_computation.1 | async-start | bytes 4194304 | tf_op jit(solution)/shard_map/all_to_all | solution.py:289
  20.2 2.3 collective-permute-start
  24.1 12.8 %shard_map.163 = (bf16[16,2,256,128]{3,2,1,0:T(8,128)(2,1)}, bf16[16,2,256,128]{3,2,1,0:T(8,128)(2,1)}) custom-call(bf16[256,4096]{1,0:T(8,128)(2,1)} %q_ref.5, bf16[256,4096]{1,0:T(8,128)(2,1)} %k_ref.5, bf16[256,4096]{1,0:T(8,128)(2,1)} %v_ref.5, bf16[256,4096]{1,0:T(8,128)(2,1)} %cot_ref.5, bf16[6,4096]{1,0:T(8,128)(2,1)} %copy-done.5, f32[3,3,4096]{2,1,0:T(4,128)} %w_ref.5), custom_call_target="tpu_custom_call" | custom-call | flops 100000000 | bytes 12000000 | tf_op jit(solution)/shard_map/pallas_call | solution.py:350
  36.9 21.8 %all-to-all-done.1.h_ref = bf16[16,2,256,128]{3,2,1,0:T(8,128)(2,1)S(1)} async-done(((bf16[16,2,256,128]{3,2,1,0:T(8,128)(2,1)}), bf16[16,2,256,128]{3,2,1,0:T(8,128)(2,1)S(1)}, u32[]{:S(2)}, u32[]{:S(2)}) %all-to-all-start.1) | async-done | bytes 2097184 | tf_op jit(solution)/shard_map/all_to_all | solution.py:289
  58.7 72.3 %all_to_all.30.xg_ref = bf16[16,2,256,128]{3,2,1,0:T(8,128)(2,1)} all-to-all(bf16[16,2,256,128]{3,2,1,0:T(8,128)(2,1)} %get-tuple-element.19), channel_id=1, replica_groups=mesh['ctx'=16,'tp'=2] {'ctx'}, dimensions={0} | all-to-all | bytes 4194304 | tf_op jit(solution)/shard_map/all_to_all | solution.py:289
  131.0 5.2 %all-to-all-start = ((bf16[16,2,256,128]{3,2,1,0:T(8,128)(2,1)}), bf16[16,2,256,128]{3,2,1,0:T(8,128)(2,1)S(1)}, u32[]{:S(2)}, u32[]{:S(2)}) async-start(bf16[16,2,256,128]{3,2,1,0:T(8,128)(2,1)} %get-tuple-element.17), calls=%async_computation | async-start | bytes 4194304 | tf_op jit(solution)/shard_map/all_to_all | solution.py:289
  136.3 2.0 broadcast_in_dim.4.cos_ref
  138.3 2.0 broadcast_in_dim.5.sin_ref
  140.3 29.0 %shard_map.166 = (bf16[16,2,256,128]{3,2,1,0:T(8,128)(2,1)}, bf16[16,256,128]{2,1,0:T(8,128)(2,1)}) custom-call(bf16[16,2,256,128]{3,2,1,0:T(8,128)(2,1)} %all_to_all.30.xg_ref, bf16[16,2,256,128]{3,2,1,0:T(8,128)(2,1)} %copy-done.2, bf16[1024,512]{1,0:T(8,128)(2,1)} %constant.14.clone.first_ref, bf16[512,1024]{1,0:T(8,128)(2,1)} %constant.15.clone.back_ref, ...), custom_call_target="tpu_custom_call" | custom-call | flops 12999999488 | bytes 16000000 | tf_op jit(solution)/shard_map/pallas_call | solution.py:163
  169.3 8.1 %all-to-all-done.xg_ref = bf16[16,2,256,128]{3,2,1,0:T(8,128)(2,1)S(1)} async-done(((bf16[16,2,256,128]{3,2,1,0:T(8,128)(2,1)}), bf16[16,2,256,128]{3,2,1,0:T(8,128)(2,1)S(1)}, u32[]{:S(2)}, u32[]{:S(2)}) %all-to-all-start) | async-done | bytes 2097184 | tf_op jit(solution)/shard_map/all_to_all | solution.py:289
  177.4 1.3 copy-done.3
  178.7 11.2 %all-to-all-start.4 = ((bf16[16,2,256,128]{3,2,1,0:T(8,128)(2,1)}), bf16[16,2,256,128]{3,2,1,0:T(8,128)(2,1)S(1)}, u32[]{:S(2)}, u32[]{:S(2)}) async-start(bf16[16,2,256,128]{3,2,1,0:T(8,128)(2,1)} %get-tuple-element.20), calls=%async_computation.4 | async-start | bytes 4194304 | tf_op jit(solution)/shard_map/all_to_all | solution.py:289
  189.9 29.1 %shard_map.165 = (bf16[16,2,256,128]{3,2,1,0:T(8,128)(2,1)}, bf16[16,256,128]{2,1,0:T(8,128)(2,1)}) custom-call(bf16[16,2,256,128]{3,2,1,0:T(8,128)(2,1)} %copy-done.3, bf16[16,2,256,128]{3,2,1,0:T(8,128)(2,1)} %copy-done.2, bf16[1024,512]{1,0:T(8,128)(2,1)} %constant.14.clone.first_ref, bf16[512,1024]{1,0:T(8,128)(2,1)} %constant.15.clone.back_ref, ...), custom_call_target="tpu_custom_call" | custom-call | flops 12999999488 | bytes 16000000 | tf_op jit(solution)/shard_map/pallas_call | solution.py:163
  219.0 12.1 %all-to-all-done.4.rest_1_ = bf16[16,2,256,128]{3,2,1,0:T(8,128)(2,1)S(1)} async-done(((bf16[16,2,256,128]{3,2,1,0:T(8,128)(2,1)}), bf16[16,2,256,128]{3,2,1,0:T(8,128)(2,1)S(1)}, u32[]{:S(2)}, u32[]{:S(2)}) %all-to-all-start.4) | async-done | bytes 2097184 | tf_op jit(solution)/shard_map/all_to_all | solution.py:289
  231.0 1.3 copy-done
  232.3 11.3 %all-to-all-start.2 = ((bf16[16,2,256,128]{3,2,1,0:T(8,128)(2,1)}), bf16[16,2,256,128]{3,2,1,0:T(8,128)(2,1)}, u32[]{:S(2)}, u32[]{:S(2)}) async-start(bf16[16,2,256,128]{3,2,1,0:T(8,128)(2,1)} %get-tuple-element.18), calls=%async_computation.2 | async-start | bytes 4194304 | tf_op jit(solution)/shard_map/all_to_all | solution.py:289
  243.6 2.7 pad_maximum_fusion
  246.4 38.4 %all-to-all-done.2.rest_0_ = bf16[16,2,256,128]{3,2,1,0:T(8,128)(2,1)} async-done(((bf16[16,2,256,128]{3,2,1,0:T(8,128)(2,1)}), bf16[16,2,256,128]{3,2,1,0:T(8,128)(2,1)}, u32[]{:S(2)}, u32[]{:S(2)}) %all-to-all-start.2) | async-done | bytes 2097184 | tf_op jit(solution)/shard_map/all_to_all | solution.py:289
  284.8 11.2 %all-to-all-start.5 = ((bf16[16,2,256,128]{3,2,1,0:T(8,128)(2,1)}), bf16[16,2,256,128]{3,2,1,0:T(8,128)(2,1)S(1)}, u32[]{:S(2)}, u32[]{:S(2)}) async-start(bf16[16,2,256,128]{3,2,1,0:T(8,128)(2,1)} %pad_maximum_fusion), calls=%async_computation.5 | async-start | bytes 4194304 | tf_op jit(solution)/shard_map/all_to_all | solution.py:289
  296.0 2.1 shard_map.167
  298.1 1.3 collective-permute-start.1
  299.4 2.1 collective-permute-done.1.behind_ref
  302.1 18.8 %shard_map.168 = (bf16[256,4096]{1,0:T(8,128)(2,1)}, bf16[256,4096]{1,0:T(8,128)(2,1)}, bf16[256,4096]{1,0:T(8,128)(2,1)}, bf16[256,4096]{1,0:T(8,128)(2,1)}, f32[3,3,4096]{2,1,0:T(4,128)}) custom-call(bf16[256,4096]{1,0:T(8,128)(2,1)} %q_ref.5, bf16[256,4096]{1,0:T(8,128)(2,1)} %k_ref.5, bf16[256,4096]{1,0:T(8,128)(2,1)} %v_ref.5, ...), custom_call_target="tpu_custom_call" | custom-call | flops 200000000 | bytes 20000000 | tf_op jit(solution)/shard_map/pallas_call | solution.py:386
  320.9 8.2 %collective-permute-start.2 = (f32[3,3,4096]{2,1,0:T(4,128)}, f32[3,3,4096]{2,1,0:T(4,128)S(1)}, u32[]{:S(2)}, u32[]{:S(2)}) collective-permute-start(f32[3,3,4096]{2,1,0:T(4,128)} %get-tuple-element.25), channel_id=1, source_target_pairs={{0,2},{2,0},{4,6},{6,4},{8,10},{10,8},{12,14},{14,12},{16,18},{18,... | collective-permute-start | bytes 442376 | tf_op jit(solution)/shard_map/ppermute | solution.py:296
  329.2 1.3 collective-permute-done.2
  331.4 19.6 %collective-permute-start.3 = (f32[3,3,4096]{2,1,0:T(4,128)S(1)}, f32[3,3,4096]{2,1,0:T(4,128)S(1)}, u32[]{:S(2)}, u32[]{:S(2)}) collective-permute-start(f32[3,3,4096]{2,1,0:T(4,128)S(1)} %add.12), channel_id=1, source_target_pairs={{0,4},{2,6},{4,0},{6,2},{8,12},{10,14},{12,8},{14,10},{16,20},{18,... | collective-permute-start | bytes 442376 | tf_op jit(solution)/shard_map/ppermute | solution.py:296
  351.1 5.4 %collective-permute-done.3 = f32[3,3,4096]{2,1,0:T(4,128)S(1)} collective-permute-done((f32[3,3,4096]{2,1,0:T(4,128)S(1)}, f32[3,3,4096]{2,1,0:T(4,128)S(1)}, u32[]{:S(2)}, u32[]{:S(2)}) %collective-permute-start.3) | collective-permute-done | bytes 147488 | tf_op jit(solution)/shard_map/ppermute | solution.py:296
  356.5 18.5 %collective-permute-start.4 = (f32[3,3,4096]{2,1,0:T(4,128)S(1)}, f32[3,3,4096]{2,1,0:T(4,128)S(1)}, u32[]{:S(2)}, u32[]{:S(2)}) collective-permute-start(f32[3,3,4096]{2,1,0:T(4,128)S(1)} %add.13), channel_id=1, source_target_pairs={{0,8},{2,10},{4,12},{6,14},{8,0},{10,2},{12,4},{14,6},{16,24},{18,... | collective-permute-start | bytes 442376 | tf_op jit(solution)/shard_map/ppermute | solution.py:296
  375.0 4.9 %collective-permute-done.4 = f32[3,3,4096]{2,1,0:T(4,128)S(1)} collective-permute-done((f32[3,3,4096]{2,1,0:T(4,128)S(1)}, f32[3,3,4096]{2,1,0:T(4,128)S(1)}, u32[]{:S(2)}, u32[]{:S(2)}) %collective-permute-start.4) | collective-permute-done | bytes 147488 | tf_op jit(solution)/shard_map/ppermute | solution.py:296
  380.9 1.3 copy-done.1
  382.3 9.6 %shard_map.169 = bf16[256,4096]{1,0:T(8,128)(2,1)} custom-call(bf16[16,2,256,128]{3,2,1,0:T(8,128)(2,1)} %copy-done.1), custom_call_target="tpu_custom_call" | custom-call | tf_op jit(solution)/shard_map/pallas_call | solution.py:398
  (27 shorter events, 7.6 us)
Async XLA Ops:
  10.2 48.5 %all-to-all-start.1 = ((bf16[16,2,256,128]{3,2,1,0:T(8,128)(2,1)}), bf16[16,2,256,128]{3,2,1,0:T(8,128)(2,1)S(1)}, u32[]{:S(2)}, u32[]{:S(2)}) async-start(bf16[16,2,256,128]{3,2,1,0:T(8,128)(2,1)} %shard_map.164), calls=%async_computation.1 | async-start | bytes 4194304 | tf_op jit(solution)/shard_map/all_to_all | solution.py:289
  20.2 3.2 collective-permute-start
  23.5 0.6 copy-start.5
  58.7 72.3 %copy-start.2 = (bf16[16,2,256,128]{3,2,1,0:T(8,128)(2,1)}, bf16[16,2,256,128]{3,2,1,0:T(8,128)(2,1)S(1)}, u32[]{:S(2)}) copy-start(bf16[16,2,256,128]{3,2,1,0:T(8,128)(2,1)S(1)} %all-to-all-done.1.h_ref) | copy-start | bytes 6291460
  131.0 5.3 %copy-start.8 = (f32[33,128]{1,0:T(8,128)S(1)}, f32[33,128]{1,0:T(8,128)}, u32[]{:S(2)}) copy-start(f32[33,128]{1,0:T(8,128)} %constant.18.clone) | copy-start | bytes 50692
  131.0 46.4 %all-to-all-start = ((bf16[16,2,256,128]{3,2,1,0:T(8,128)(2,1)}), bf16[16,2,256,128]{3,2,1,0:T(8,128)(2,1)S(1)}, u32[]{:S(2)}, u32[]{:S(2)}) async-start(bf16[16,2,256,128]{3,2,1,0:T(8,128)(2,1)} %get-tuple-element.17), calls=%async_computation | async-start | bytes 4194304 | tf_op jit(solution)/shard_map/all_to_all | solution.py:289
  136.3 2.0 copy-start.7
  177.4 1.3 copy-start.3
  178.7 52.3 %all-to-all-start.4 = ((bf16[16,2,256,128]{3,2,1,0:T(8,128)(2,1)}), bf16[16,2,256,128]{3,2,1,0:T(8,128)(2,1)S(1)}, u32[]{:S(2)}, u32[]{:S(2)}) async-start(bf16[16,2,256,128]{3,2,1,0:T(8,128)(2,1)} %get-tuple-element.20), calls=%async_computation.4 | async-start | bytes 4194304 | tf_op jit(solution)/shard_map/all_to_all | solution.py:289
  231.0 1.3 copy-start
  231.0 12.6 %copy-start.4 = (bf16[16,256,128]{2,1,0:T(8,128)(2,1)S(1)}, bf16[16,256,128]{2,1,0:T(8,128)(2,1)}, u32[]{:S(2)}) copy-start(bf16[16,256,128]{2,1,0:T(8,128)(2,1)} %get-tuple-element.27) | copy-start | bytes 3145732
  232.3 52.4 %all-to-all-start.2 = ((bf16[16,2,256,128]{3,2,1,0:T(8,128)(2,1)}), bf16[16,2,256,128]{3,2,1,0:T(8,128)(2,1)}, u32[]{:S(2)}, u32[]{:S(2)}) async-start(bf16[16,2,256,128]{3,2,1,0:T(8,128)(2,1)} %get-tuple-element.18), calls=%async_computation.2 | async-start | bytes 4194304 | tf_op jit(solution)/shard_map/all_to_all | solution.py:289
  284.8 96.2 %all-to-all-start.5 = ((bf16[16,2,256,128]{3,2,1,0:T(8,128)(2,1)}), bf16[16,2,256,128]{3,2,1,0:T(8,128)(2,1)S(1)}, u32[]{:S(2)}, u32[]{:S(2)}) async-start(bf16[16,2,256,128]{3,2,1,0:T(8,128)(2,1)} %pad_maximum_fusion), calls=%async_computation.5 | async-start | bytes 4194304 | tf_op jit(solution)/shard_map/all_to_all | solution.py:289
  298.1 3.3 collective-permute-start.1
  301.5 0.6 copy-start.6
  320.9 9.5 %collective-permute-start.2 = (f32[3,3,4096]{2,1,0:T(4,128)}, f32[3,3,4096]{2,1,0:T(4,128)S(1)}, u32[]{:S(2)}, u32[]{:S(2)}) collective-permute-start(f32[3,3,4096]{2,1,0:T(4,128)} %get-tuple-element.25), channel_id=1, source_target_pairs={{0,2},{2,0},{4,6},{6,4},{8,10},{10,8},{12,14},{14,12},{16,18},{18,... | collective-permute-start | bytes 442376 | tf_op jit(solution)/shard_map/ppermute | solution.py:296
  331.4 25.1 %collective-permute-start.3 = (f32[3,3,4096]{2,1,0:T(4,128)S(1)}, f32[3,3,4096]{2,1,0:T(4,128)S(1)}, u32[]{:S(2)}, u32[]{:S(2)}) collective-permute-start(f32[3,3,4096]{2,1,0:T(4,128)S(1)} %add.12), channel_id=1, source_target_pairs={{0,4},{2,6},{4,0},{6,2},{8,12},{10,14},{12,8},{14,10},{16,20},{18,... | collective-permute-start | bytes 442376 | tf_op jit(solution)/shard_map/ppermute | solution.py:296
  356.5 23.3 %collective-permute-start.4 = (f32[3,3,4096]{2,1,0:T(4,128)S(1)}, f32[3,3,4096]{2,1,0:T(4,128)S(1)}, u32[]{:S(2)}, u32[]{:S(2)}) collective-permute-start(f32[3,3,4096]{2,1,0:T(4,128)S(1)} %add.13), channel_id=1, source_target_pairs={{0,8},{2,10},{4,12},{6,14},{8,0},{10,2},{12,4},{14,6},{16,24},{18,... | collective-permute-start | bytes 442376 | tf_op jit(solution)/shard_map/ppermute | solution.py:296
  379.9 11.9 %collective-permute-start.5 = (f32[3,3,4096]{2,1,0:T(4,128)S(1)}, f32[3,3,4096]{2,1,0:T(4,128)S(1)}, u32[]{:S(2)}, u32[]{:S(2)}) collective-permute-start(f32[3,3,4096]{2,1,0:T(4,128)S(1)} %add.14), channel_id=1, source_target_pairs={{0,16},{2,18},{4,20},{6,22},{8,24},{10,26},{12,28},{14,30},{16,0},... | collective-permute-start | bytes 442376 | tf_op jit(solution)/shard_map/ppermute | solution.py:296
  380.9 1.3 copy-start.1

commit v3 on v2

--- a/solution.py
+++ b/solution.py
@@ -45,9 +45,7 @@
 def spectral_kernel(
     inv_root,
     scale,
-    chunk,
     xg_ref,
-    h_ref,
     first_ref,
     back_ref,
     inner_fwd_ref,
@@ -60,7 +58,7 @@
 ):
     k_count = work.shape[0]
     half_rows = k_count - 1
-    rows_per = h_ref.shape[2] // S
+    rows_per = xg_ref.shape[2] // S
 
     def first_section(step, carry):
         at = pl.multiple_of(step * G, G)
@@ -72,7 +70,7 @@
                     [
                         xg_ref[r // rows_per, 0, rows, :],
                         xg_ref[r // rows_per, 1, rows, :],
-                        h_ref[r // rows_per, chunk, rows, :],
+                        xg_ref[r // rows_per, 2, rows, :],
                     ],
                     axis=1,
                 )
@@ -154,26 +152,25 @@
     lax.fori_loop(0, S // G, last_section, 0)
 
 
-def transform_chunk(xg, h, chunk, tables, inv_root, scale):
+def transform_chunk(xg, tables, inv_root, scale):
     k_count = tables[4].shape[0]
-    lanes = h.shape[-1]
+    lanes = xg.shape[-1]
     if lanes < LANES:
         xg = jnp.pad(xg, ((0, 0),) * 3 + ((0, LANES - lanes),))
-        h = jnp.pad(h, ((0, 0),) * 3 + ((0, LANES - lanes),))
     cg, gf = pl.pallas_call(
-        functools.partial(spectral_kernel, inv_root, scale, chunk),
+        functools.partial(spectral_kernel, inv_root, scale),
         out_shape=(
-            jax.ShapeDtypeStruct(xg.shape, jnp.bfloat16),
-            jax.ShapeDtypeStruct((h.shape[0],) + h.shape[2:], jnp.bfloat16),
-        ),
-        in_specs=[pl.BlockSpec(memory_space=pltpu.VMEM)] * 8,
+            jax.ShapeDtypeStruct((xg.shape[0], 2) + xg.shape[2:], jnp.bfloat16),
+            jax.ShapeDtypeStruct(xg.shape[:1] + xg.shape[2:], jnp.bfloat16),
+        ),
+        in_specs=[pl.BlockSpec(memory_space=pltpu.VMEM)] * 7,
         out_specs=(pl.BlockSpec(memory_space=pltpu.VMEM),) * 2,
         scratch_shapes=[pltpu.VMEM((k_count, 2 * S, 3 * LANES), jnp.bfloat16)],
         compiler_params=pltpu.CompilerParams(vmem_limit_bytes=58 * 1024 * 1024),
         cost_estimate=pl.CostEstimate(
             flops=13_000_000_000, bytes_accessed=16_000_000, transcendentals=0
         ),
-    )(xg, h, *tables)
+    )(xg, *tables)
     return cg[..., :lanes], gf[..., :lanes]
 
 
@@ -208,14 +205,6 @@
     return x.astype(jnp.bfloat16)
 
 
-def filter_kernel(h_ref, out_ref):
-    per, chunks, _, lanes = out_ref.shape
-    for i in range(per):
-        for c in range(chunks):
-            at = (i * chunks + c) * lanes
-            out_ref[i, c] = h_ref[:, at : at + lanes]
-
-
 def unpack_kernel(gf_ref, out_ref):
     per, chunks, _, lanes = gf_ref.shape
     for i in range(per):
@@ -224,7 +213,7 @@
             out_ref[:, at : at + lanes] = gf_ref[i, c]
 
 
-def entry_kernel(q_ref, k_ref, v_ref, cot_ref, ahead_ref, w_ref, *outs):
+def entry_kernel(q_ref, k_ref, v_ref, cot_ref, ahead_ref, w_ref, h_ref, *outs):
     ahead = as_float(ahead_ref)
     per, _, _, lanes = outs[0].shape
     shorts = []
@@ -237,6 +226,7 @@
             at = (i * len(outs) + c) * lanes
             out[i, 0] = mixed[:, at : at + lanes]
             out[i, 1] = grad_conv[:, at : at + lanes]
+            out[i, 2] = h_ref[:, at : at + lanes]
 
 
 def local_grads(q_ref, k_ref, v_ref, cot_ref, ahead_ref, w_ref, conv, grad_mixed):
@@ -291,10 +281,18 @@
 
 def sum_over(x, axis):
     count = lax.axis_size(axis)
+
+    def partner(y, flip):
+        return lax.ppermute(y, axis, [(i, i ^ flip) for i in range(count)])
+
     step = 1
     while step < count:
-        x = x + lax.ppermute(x, axis, [(i, i ^ step) for i in range(count)])
-        step *= 2
+        if 2 * step < count:
+            x = (x + partner(x, step)) + (partner(x, 2 * step) + partner(x, 3 * step))
+            step *= 4
+        else:
+            x = x + partner(x, step)
+            step *= 2
     return x
 
 
@@ -318,6 +316,7 @@
     rim = pl.BlockSpec((3 * rim_rows, width), lambda i: (0, i))
     taps = pl.BlockSpec((3, tap_count, width), lambda i: (0, 0, i))
     pair = pl.BlockSpec((per, 2, local_rows, lanes), lambda i: (i, 0, 0, 0))
+    triple = pl.BlockSpec((per, 3, local_rows, lanes), lambda i: (i, 0, 0, 0))
     packed = pl.BlockSpec((per, chunks, local_rows, lanes), lambda i: (i, 0, 0, 0))
     whole = jax.ShapeDtypeStruct((local_rows, channels), jnp.bfloat16)
 
@@ -336,35 +335,25 @@
     )
     tails = jnp.concatenate([x[local_rows - rim_rows :] for x in (query_in, key_in, value_in)])
     ahead = from_behind(tails, "ctx", 1)
-    h = exchange(
-        pl.pallas_call(
-            filter_kernel,
-            grid=(steps,),
-            out_shape=jax.ShapeDtypeStruct((ctx_size, chunks, local_rows, lanes), jnp.bfloat16),
-            in_specs=[stream],
-            out_specs=packed,
-            compiler_params=limit,
-        )(long_filter)
-    )
     streams = (query_in, key_in, value_in, cotangent, ahead, short_weight)
     xg_parts = pl.pallas_call(
         entry_kernel,
         grid=(steps,),
         out_shape=(
-            jax.ShapeDtypeStruct((ctx_size, 2, local_rows, lanes), jnp.bfloat16),
+            jax.ShapeDtypeStruct((ctx_size, 3, local_rows, lanes), jnp.bfloat16),
         )
         * chunks,
-        in_specs=[stream] * 4 + [rim, taps],
-        out_specs=(pair,) * chunks,
+        in_specs=[stream] * 4 + [rim, taps, stream],
+        out_specs=(triple,) * chunks,
         compiler_params=limit,
         cost_estimate=pl.CostEstimate(
             flops=100_000_000, bytes_accessed=12_000_000, transcendentals=0
         ),
-    )(*streams)
+    )(*streams, long_filter)
     xg_parts = [exchange(xg) for xg in xg_parts]
     cg_parts, gf_parts = [], []
-    for c, xg in enumerate(xg_parts):
-        cg, gf = transform_chunk(xg, h, c, tables, inv_root, 1.0 / fft_size)
+    for xg in xg_parts:
+        cg, gf = transform_chunk(xg, tables, inv_root, 1.0 / fft_size)
         cg_parts.append(exchange(cg))
         gf_parts.append(gf)
     gf_back = exchange(jnp.stack(gf_parts, axis=1))
@@ -394,6 +383,7 @@
             flops=200_000_000, bytes_accessed=20_000_000, transcendentals=0
         ),
     )(*streams, behind, *cg_parts)
+    short_part, gf_back = lax.optimization_barrier((short_part, gf_back))
     grad_short = sum_over(short_part, "ctx") * inv_root
     grad_filter = pl.pallas_call(
         unpack_kernel,

time: 395 us -> 385 us (0.975)
  starting transfers between devices: 97.3 us -> 78.2 us
  waiting for transfers between devices: 94.9 us -> 108 us
  Pallas kernels: 111 us -> 102 us
  blocking collectives: 72.3 us -> 79.6 us
    ppermute x4 -> x6, starting transfers between devices: 47.4 us -> 31.3 us  [partner(): return lax.ppermute(y, axis, [(i, i ^ flip) for i in range(count)])]
    all_to_all x5 -> x4, waiting for transfers between devices: 80.4 us -> 93.5 us  [exchange(): return lax.all_to_all(x, 'ctx', split_axis=0, concat_axis=0, tiled=True)]
    pallas_call x3 -> x2, Pallas kernels: 67.6 us -> 57.5 us  [transform_chunk(): pl.pallas_call(functools.partial(spectral_kernel, inv_root, scale), out_s...]
    all_to_all x1, blocking collectives: 72.3 us -> 79.6 us  [exchange(): return lax.all_to_all(x, 'ctx', split_axis=0, concat_axis=0, tiled=True)]
    all_to_all x5 -> x4, starting transfers between devices: 46.3 us -> 43.2 us  [exchange(): return lax.all_to_all(x, 'ctx', split_axis=0, concat_axis=0, tiled=True)]
    ppermute x4 -> x6, waiting for transfers between devices: 11.6 us -> 11.1 us  [partner(): return lax.ppermute(y, axis, [(i, i ^ flip) for i in range(count)])]
  transfers between devices with their start and end apart: 11 -> 12, of which waited for: 9 -> 9; matrix products, arithmetic and copies ran while one was open for 3% -> 2% of each run, Pallas kernels for 26% -> 23%
where the time goes in v3:
time: 385 us; the launch traced here: 383 us
  waiting for transfers between devices  108 us (28%)
  Pallas kernels  102 us (26%)
  blocking collectives  79.6 us (21%)
  starting transfers between devices  78.2 us (20%)
  local copies, waits for them, and re-layouts  10.8 us (3%)
  other arithmetic  4.61 us (1%)
    all_to_all x4, waiting for transfers between devices, exchange(): return lax.all_to_all(x, 'ctx', split_axis=0, concat_axis=0, tiled=True)  93.5 us
    all_to_all x1, blocking collectives, exchange(): return lax.all_to_all(x, 'ctx', split_axis=0, concat_axis=0, tiled=True)  79.6 us
    pallas_call x2, Pallas kernels, transform_chunk(): pl.pallas_call(functools.partial(spectral_kernel, inv_root, scale), out_s...  57.5 us
    all_to_all x4, starting transfers between devices, exchange(): return lax.all_to_all(x, 'ctx', split_axis=0, concat_axis=0, tiled=True)  43.2 us
    ppermute x6, starting transfers between devices, partner(): return lax.ppermute(y, axis, [(i, i ^ flip) for i in range(count)])  31.3 us
    pallas_call x1, Pallas kernels, on_device(): pl.pallas_call(functools.partial(exit_kernel, chunks), grid=(steps,), out...  18.8 us
    pallas_call x1, Pallas kernels, on_device(): pl.pallas_call(entry_kernel, grid=(steps,), out_shape=(jax.ShapeDtypeStru...  13.7 us
    ppermute x6, waiting for transfers between devices, partner(): return lax.ppermute(y, axis, [(i, i ^ flip) for i in range(count)])  11.1 us
  transfers between devices with their start and end apart: 12, of which 9 were waited for; matrix products, arithmetic and copies ran while one was open for 2% of the time, Pallas kernels for 23%

profile of v3, /device:TPU:0, one launch (start us, length us, event | category | flops | bytes accessed | tf_op | source)
XLA Modules:
  0.0 383.2 jit_solution(114321913108133207)
XLA Ops:
  0.6 0.9 slice.9
  3.3 2.4 collective-permute-start
  5.7 0.9 collective-permute-done.ahead_ref
  7.2 13.7 %shard_map.163 = (bf16[16,3,256,128]{3,2,1,0:T(8,128)(2,1)}, bf16[16,3,256,128]{3,2,1,0:T(8,128)(2,1)}) custom-call(bf16[256,4096]{1,0:T(8,128)(2,1)} %q_ref.5, bf16[256,4096]{1,0:T(8,128)(2,1)} %k_ref.5, bf16[256,4096]{1,0:T(8,128)(2,1)} %v_ref.5, bf16[256,4096]{1,0:T(8,128)(2,1)} %cot_ref.5, bf16[6,4096]{1,0:T(8,128)(2,1)} %copy-done.4, ...), custom_call_target="tpu_custom_call" | custom-call | flops 100000000 | bytes 12000000 | tf_op jit(solution)/shard_map/pallas_call | solution.py:339
  20.9 79.6 %all_to_all.25.xg_ref = bf16[16,3,256,128]{3,2,1,0:T(8,128)(2,1)} all-to-all(bf16[16,3,256,128]{3,2,1,0:T(8,128)(2,1)} %get-tuple-element.19), channel_id=1, replica_groups=mesh['ctx'=16,'tp'=2] {'ctx'}, dimensions={0} | all-to-all | bytes 6291456 | tf_op jit(solution)/shard_map/all_to_all | solution.py:279
  100.5 5.3 %all-to-all-start.2 = ((bf16[16,3,256,128]{3,2,1,0:T(8,128)(2,1)}), bf16[16,3,256,128]{3,2,1,0:T(8,128)(2,1)S(1)}, u32[]{:S(2)}, u32[]{:S(2)}) async-start(bf16[16,3,256,128]{3,2,1,0:T(8,128)(2,1)} %get-tuple-element.21), calls=%async_computation.2 | async-start | bytes 6291456 | tf_op jit(solution)/shard_map/all_to_all | solution.py:279
  105.8 2.0 broadcast_in_dim.4.cos_ref
  107.9 2.0 broadcast_in_dim.5.sin_ref
  109.9 28.7 %shard_map.164 = (bf16[16,2,256,128]{3,2,1,0:T(8,128)(2,1)}, bf16[16,256,128]{2,1,0:T(8,128)(2,1)}) custom-call(bf16[16,3,256,128]{3,2,1,0:T(8,128)(2,1)} %all_to_all.25.xg_ref, bf16[1024,512]{1,0:T(8,128)(2,1)} %constant.14.clone.first_ref, bf16[512,1024]{1,0:T(8,128)(2,1)} %constant.15.clone.back_ref, bf16[256,256]{1,0:T(8,128)(2,1)} %constant.16.clone.inner_fwd_ref, ...), custom_call_target="tpu_custom_call" | custom-call | flops 12999999488 | bytes 16000000 | tf_op jit(solution)/shard_map/pallas_call | solution.py:160
  138.6 26.6 %all-to-all-done.2.xg_ref = bf16[16,3,256,128]{3,2,1,0:T(8,128)(2,1)S(1)} async-done(((bf16[16,3,256,128]{3,2,1,0:T(8,128)(2,1)}), bf16[16,3,256,128]{3,2,1,0:T(8,128)(2,1)S(1)}, u32[]{:S(2)}, u32[]{:S(2)}) %all-to-all-start.2) | async-done | bytes 3145760 | tf_op jit(solution)/shard_map/all_to_all | solution.py:279
  165.2 1.6 copy-done.2
  166.8 15.4 %all-to-all-start.1 = ((bf16[16,2,256,128]{3,2,1,0:T(8,128)(2,1)}), bf16[16,2,256,128]{3,2,1,0:T(8,128)(2,1)S(1)}, u32[]{:S(2)}, u32[]{:S(2)}) async-start(bf16[16,2,256,128]{3,2,1,0:T(8,128)(2,1)} %get-tuple-element.20), calls=%async_computation.1 | async-start | bytes 4194304 | tf_op jit(solution)/shard_map/all_to_all | solution.py:279
  182.2 28.7 %shard_map.165 = (bf16[16,2,256,128]{3,2,1,0:T(8,128)(2,1)}, bf16[16,256,128]{2,1,0:T(8,128)(2,1)}) custom-call(bf16[16,3,256,128]{3,2,1,0:T(8,128)(2,1)} %copy-done.2, bf16[1024,512]{1,0:T(8,128)(2,1)} %constant.14.clone.first_ref, bf16[512,1024]{1,0:T(8,128)(2,1)} %constant.15.clone.back_ref, bf16[256,256]{1,0:T(8,128)(2,1)} %constant.16.clone.inner_fwd_ref, ...), custom_call_target="tpu_custom_call" | custom-call | flops 12999999488 | bytes 16000000 | tf_op jit(solution)/shard_map/pallas_call | solution.py:160
  211.0 12.4 %all-to-all-done.1.rest_0_ = bf16[16,2,256,128]{3,2,1,0:T(8,128)(2,1)S(1)} async-done(((bf16[16,2,256,128]{3,2,1,0:T(8,128)(2,1)}), bf16[16,2,256,128]{3,2,1,0:T(8,128)(2,1)S(1)}, u32[]{:S(2)}, u32[]{:S(2)}) %all-to-all-start.1) | async-done | bytes 2097184 | tf_op jit(solution)/shard_map/all_to_all | solution.py:279
  223.3 1.3 copy-done
  224.7 11.3 %all-to-all-start.3 = ((bf16[16,2,256,128]{3,2,1,0:T(8,128)(2,1)}), bf16[16,2,256,128]{3,2,1,0:T(8,128)(2,1)}, u32[]{:S(2)}, u32[]{:S(2)}) async-start(bf16[16,2,256,128]{3,2,1,0:T(8,128)(2,1)} %get-tuple-element.22), calls=%async_computation.3 | async-start | bytes 4194304 | tf_op jit(solution)/shard_map/all_to_all | solution.py:279
  235.9 2.8 pad_maximum_fusion
  238.7 38.4 %all-to-all-done.3.rest_1_ = bf16[16,2,256,128]{3,2,1,0:T(8,128)(2,1)} async-done(((bf16[16,2,256,128]{3,2,1,0:T(8,128)(2,1)}), bf16[16,2,256,128]{3,2,1,0:T(8,128)(2,1)}, u32[]{:S(2)}, u32[]{:S(2)}) %all-to-all-start.3) | async-done | bytes 2097184 | tf_op jit(solution)/shard_map/all_to_all | solution.py:279
  277.1 11.2 %all-to-all-start.4 = ((bf16[16,2,256,128]{3,2,1,0:T(8,128)(2,1)}), bf16[16,2,256,128]{3,2,1,0:T(8,128)(2,1)S(1)}, u32[]{:S(2)}, u32[]{:S(2)}) async-start(bf16[16,2,256,128]{3,2,1,0:T(8,128)(2,1)} %pad_maximum_fusion), calls=%async_computation.4 | async-start | bytes 4194304 | tf_op jit(solution)/shard_map/all_to_all | solution.py:279
  288.3 2.1 shard_map.166
  290.4 1.3 collective-permute-start.1
  291.7 2.1 collective-permute-done.1.behind_ref
  294.4 18.8 %shard_map.167 = (bf16[256,4096]{1,0:T(8,128)(2,1)}, bf16[256,4096]{1,0:T(8,128)(2,1)}, bf16[256,4096]{1,0:T(8,128)(2,1)}, bf16[256,4096]{1,0:T(8,128)(2,1)}, f32[3,3,4096]{2,1,0:T(4,128)}) custom-call(bf16[256,4096]{1,0:T(8,128)(2,1)} %q_ref.5, bf16[256,4096]{1,0:T(8,128)(2,1)} %k_ref.5, bf16[256,4096]{1,0:T(8,128)(2,1)} %v_ref.5, ...), custom_call_target="tpu_custom_call" | custom-call | flops 200000000 | bytes 20000000 | tf_op jit(solution)/shard_map/pallas_call | solution.py:375
  313.2 16.2 %all-to-all-done.4.gf_ref = bf16[16,2,256,128]{3,2,1,0:T(8,128)(2,1)S(1)} async-done(((bf16[16,2,256,128]{3,2,1,0:T(8,128)(2,1)}), bf16[16,2,256,128]{3,2,1,0:T(8,128)(2,1)S(1)}, u32[]{:S(2)}, u32[]{:S(2)}) %all-to-all-start.4) | async-done | bytes 2097184 | tf_op jit(solution)/shard_map/all_to_all | solution.py:279
  329.4 11.2 %collective-permute-start.4 = (f32[3,3,4096]{2,1,0:T(4,128)}, f32[3,3,4096]{2,1,0:T(4,128)S(1)}, u32[]{:S(2)}, u32[]{:S(2)}) collective-permute-start(f32[3,3,4096]{2,1,0:T(4,128)} %get-tuple-element.30), channel_id=1, source_target_pairs={{0,6},{2,4},{4,2},{6,0},{8,14},{10,12},{12,10},{14,8},{16,22},{18,... | collective-permute-start | bytes 442376 | tf_op jit(solution)/shard_map/ppermute | solution.py:286
  340.8 4.9 %collective-permute-done.4 = f32[3,3,4096]{2,1,0:T(4,128)S(1)} collective-permute-done((f32[3,3,4096]{2,1,0:T(4,128)}, f32[3,3,4096]{2,1,0:T(4,128)S(1)}, u32[]{:S(2)}, u32[]{:S(2)}) %collective-permute-start.4) | collective-permute-done | bytes 147488 | tf_op jit(solution)/shard_map/ppermute | solution.py:286
  345.7 2.7 collective-permute-done.3
  348.4 1.0 add_add_fusion
  349.4 6.6 %collective-permute-start.7 = (f32[3,3,4096]{2,1,0:T(4,128)S(1)}, f32[3,3,4096]{2,1,0:T(4,128)S(1)}, u32[]{:S(2)}, u32[]{:S(2)}) collective-permute-start(f32[3,3,4096]{2,1,0:T(4,128)S(1)} %add_add_fusion), channel_id=1, source_target_pairs={{0,24},{2,26},{4,28},{6,30},{8,16},{10,18},{12,20},{14,22},{16,8},... | collective-permute-start | bytes 442376 | tf_op jit(solution)/shard_map/ppermute | solution.py:286
  356.1 13.3 %collective-permute-start.6 = (f32[3,3,4096]{2,1,0:T(4,128)S(1)}, f32[3,3,4096]{2,1,0:T(4,128)S(1)}, u32[]{:S(2)}, u32[]{:S(2)}) collective-permute-start(f32[3,3,4096]{2,1,0:T(4,128)S(1)} %add_add_fusion), channel_id=1, source_target_pairs={{0,16},{2,18},{4,20},{6,22},{8,24},{10,26},{12,28},{14,30},{16,0},... | collective-permute-start | bytes 442376 | tf_op jit(solution)/shard_map/ppermute | solution.py:286
  369.4 9.6 %shard_map.168 = bf16[256,4096]{1,0:T(8,128)(2,1)} custom-call(bf16[16,2,256,128]{3,2,1,0:T(8,128)(2,1)} %copy-done.1), custom_call_target="tpu_custom_call" | custom-call | tf_op jit(solution)/shard_map/pallas_call | solution.py:388
  378.9 3.5 collective-permute-done.6
  (24 shorter events, 4.0 us)
Async XLA Ops:
  3.3 3.2 collective-permute-start
  6.5 0.6 copy-start.4
  100.5 5.3 %copy-start.7 = (f32[33,128]{1,0:T(8,128)S(1)}, f32[33,128]{1,0:T(8,128)}, u32[]{:S(2)}) copy-start(f32[33,128]{1,0:T(8,128)} %constant.18.clone) | copy-start | bytes 50692
  100.5 64.7 %all-to-all-start.2 = ((bf16[16,3,256,128]{3,2,1,0:T(8,128)(2,1)}), bf16[16,3,256,128]{3,2,1,0:T(8,128)(2,1)S(1)}, u32[]{:S(2)}, u32[]{:S(2)}) async-start(bf16[16,3,256,128]{3,2,1,0:T(8,128)(2,1)} %get-tuple-element.21), calls=%async_computation.2 | async-start | bytes 6291456 | tf_op jit(solution)/shard_map/all_to_all | solution.py:279
  105.8 2.0 copy-start.6
  165.2 1.6 copy-start.2
  166.8 56.5 %all-to-all-start.1 = ((bf16[16,2,256,128]{3,2,1,0:T(8,128)(2,1)}), bf16[16,2,256,128]{3,2,1,0:T(8,128)(2,1)S(1)}, u32[]{:S(2)}, u32[]{:S(2)}) async-start(bf16[16,2,256,128]{3,2,1,0:T(8,128)(2,1)} %get-tuple-element.20), calls=%async_computation.1 | async-start | bytes 4194304 | tf_op jit(solution)/shard_map/all_to_all | solution.py:279
  223.3 1.3 copy-start
  223.3 12.6 %copy-start.3 = (bf16[16,256,128]{2,1,0:T(8,128)(2,1)S(1)}, bf16[16,256,128]{2,1,0:T(8,128)(2,1)}, u32[]{:S(2)}) copy-start(bf16[16,256,128]{2,1,0:T(8,128)(2,1)} %get-tuple-element.28) | copy-start | bytes 3145732
  224.7 52.4 %all-to-all-start.3 = ((bf16[16,2,256,128]{3,2,1,0:T(8,128)(2,1)}), bf16[16,2,256,128]{3,2,1,0:T(8,128)(2,1)}, u32[]{:S(2)}, u32[]{:S(2)}) async-start(bf16[16,2,256,128]{3,2,1,0:T(8,128)(2,1)} %get-tuple-element.22), calls=%async_computation.3 | async-start | bytes 4194304 | tf_op jit(solution)/shard_map/all_to_all | solution.py:279
  277.1 52.3 %all-to-all-start.4 = ((bf16[16,2,256,128]{3,2,1,0:T(8,128)(2,1)}), bf16[16,2,256,128]{3,2,1,0:T(8,128)(2,1)S(1)}, u32[]{:S(2)}, u32[]{:S(2)}) async-start(bf16[16,2,256,128]{3,2,1,0:T(8,128)(2,1)} %pad_maximum_fusion), calls=%async_computation.4 | async-start | bytes 4194304 | tf_op jit(solution)/shard_map/all_to_all | solution.py:279
  290.4 3.3 collective-permute-start.1
  293.8 0.6 copy-start.5
  329.4 40.0 %copy-start.1 = (bf16[16,2,256,128]{3,2,1,0:T(8,128)(2,1)}, bf16[16,2,256,128]{3,2,1,0:T(8,128)(2,1)S(1)}, u32[]{:S(2)}) copy-start(bf16[16,2,256,128]{3,2,1,0:T(8,128)(2,1)S(1)} %all-to-all-done.4.gf_ref) | copy-start | bytes 6291460
  329.4 16.3 %collective-permute-start.4 = (f32[3,3,4096]{2,1,0:T(4,128)}, f32[3,3,4096]{2,1,0:T(4,128)S(1)}, u32[]{:S(2)}, u32[]{:S(2)}) collective-permute-start(f32[3,3,4096]{2,1,0:T(4,128)} %get-tuple-element.30), channel_id=1, source_target_pairs={{0,6},{2,4},{4,2},{6,0},{8,14},{10,12},{12,10},{14,8},{16,22},{18,... | collective-permute-start | bytes 442376 | tf_op jit(solution)/shard_map/ppermute | solution.py:286
  340.6 7.8 %collective-permute-start.3 = (f32[3,3,4096]{2,1,0:T(4,128)}, f32[3,3,4096]{2,1,0:T(4,128)S(1)}, u32[]{:S(2)}, u32[]{:S(2)}) collective-permute-start(f32[3,3,4096]{2,1,0:T(4,128)} %get-tuple-element.30), channel_id=1, source_target_pairs={{0,4},{2,6},{4,0},{6,2},{8,12},{10,14},{12,8},{14,10},{16,20},{18,... | collective-permute-start | bytes 442376 | tf_op jit(solution)/shard_map/ppermute | solution.py:286
  340.6 7.8 %collective-permute-start.2 = (f32[3,3,4096]{2,1,0:T(4,128)}, f32[3,3,4096]{2,1,0:T(4,128)S(1)}, u32[]{:S(2)}, u32[]{:S(2)}) collective-permute-start(f32[3,3,4096]{2,1,0:T(4,128)} %get-tuple-element.30), channel_id=1, source_target_pairs={{0,2},{2,0},{4,6},{6,4},{8,10},{10,8},{12,14},{14,12},{16,18},{18,... | collective-permute-start | bytes 442376 | tf_op jit(solution)/shard_map/ppermute | solution.py:286
  349.4 29.5 %collective-permute-start.7 = (f32[3,3,4096]{2,1,0:T(4,128)S(1)}, f32[3,3,4096]{2,1,0:T(4,128)S(1)}, u32[]{:S(2)}, u32[]{:S(2)}) collective-permute-start(f32[3,3,4096]{2,1,0:T(4,128)S(1)} %add_add_fusion), channel_id=1, source_target_pairs={{0,24},{2,26},{4,28},{6,30},{8,16},{10,18},{12,20},{14,22},{16,8},... | collective-permute-start | bytes 442376 | tf_op jit(solution)/shard_map/ppermute | solution.py:286
  356.1 26.4 %collective-permute-start.6 = (f32[3,3,4096]{2,1,0:T(4,128)S(1)}, f32[3,3,4096]{2,1,0:T(4,128)S(1)}, u32[]{:S(2)}, u32[]{:S(2)}) collective-permute-start(f32[3,3,4096]{2,1,0:T(4,128)S(1)} %add_add_fusion), channel_id=1, source_target_pairs={{0,16},{2,18},{4,20},{6,22},{8,24},{10,26},{12,28},{14,30},{16,0},... | collective-permute-start | bytes 442376 | tf_op jit(solution)/shard_map/ppermute | solution.py:286
  369.4 13.0 %collective-permute-start.5 = (f32[3,3,4096]{2,1,0:T(4,128)S(1)}, f32[3,3,4096]{2,1,0:T(4,128)S(1)}, u32[]{:S(2)}, u32[]{:S(2)}) collective-permute-start(f32[3,3,4096]{2,1,0:T(4,128)S(1)} %add_add_fusion), channel_id=1, source_target_pairs={{0,8},{2,10},{4,12},{6,14},{8,0},{10,2},{12,4},{14,6},{16,24},{18,... | collective-permute-start | bytes 442376 | tf_op jit(solution)/shard_map/ppermute | solution.py:286

commit v4 on v3

--- a/solution.py
+++ b/solution.py
@@ -279,21 +279,13 @@
     return lax.all_to_all(x, "ctx", split_axis=0, concat_axis=0, tiled=True)
 
 
-def sum_over(x, axis):
-    count = lax.axis_size(axis)
-
-    def partner(y, flip):
-        return lax.ppermute(y, axis, [(i, i ^ flip) for i in range(count)])
-
-    step = 1
-    while step < count:
-        if 2 * step < count:
-            x = (x + partner(x, step)) + (partner(x, 2 * step) + partner(x, 3 * step))
-            step *= 4
-        else:
-            x = x + partner(x, step)
-            step *= 2
-    return x
+def sum_over(x):
+    rows, channels = x.shape
+    count = lax.axis_size("ctx")
+    terms = exchange(x.reshape(rows, count, channels // count).transpose(1, 0, 2))
+    total = jnp.sum(terms, axis=0)
+    totals = exchange(jnp.broadcast_to(total[None], terms.shape))
+    return totals.transpose(1, 0, 2).reshape(rows, channels)
 
 
 def on_device(query_in, key_in, value_in, cotangent, short_weight, long_filter):
@@ -383,8 +375,8 @@
             flops=200_000_000, bytes_accessed=20_000_000, transcendentals=0
         ),
     )(*streams, behind, *cg_parts)
-    short_part, gf_back = lax.optimization_barrier((short_part, gf_back))
-    grad_short = sum_over(short_part, "ctx") * inv_root
+    short_total = sum_over(short_part.reshape(3 * tap_count, channels))
+    grad_short = short_total.reshape(3, tap_count, channels) * inv_root
     grad_filter = pl.pallas_call(
         unpack_kernel,
         grid=(steps,),

time: 385 us -> 396 us (1.029)
  blocking collectives: 79.6 us -> 138 us
  starting transfers between devices: 78.2 us -> 46.4 us
  waiting for transfers between devices: 108 us -> 92.1 us
    all_to_all x1 -> x2, blocking collectives: 79.6 us -> 138 us  [exchange(): return lax.all_to_all(x, 'ctx', split_axis=0, concat_axis=0, tiled=True)]
    ppermute x6 -> x0, starting transfers between devices: 31.3 us -> none  [partner(): return lax.ppermute(y, axis, [(i, i ^ flip) for i in range(count)])]
    ppermute x6 -> x0, waiting for transfers between devices: 11.1 us -> none  [partner(): return lax.ppermute(y, axis, [(i, i ^ flip) for i in range(count)])]
    all_to_all x4 -> x5, waiting for transfers between devices: 93.5 us -> 88.9 us  [exchange(): return lax.all_to_all(x, 'ctx', split_axis=0, concat_axis=0, tiled=True)]
    all_to_all x4 -> x5, starting transfers between devices: 43.2 us -> 42.7 us  [exchange(): return lax.all_to_all(x, 'ctx', split_axis=0, concat_axis=0, tiled=True)]
  transfers between devices with their start and end apart: 12 -> 7, of which waited for: 9 -> 7; matrix products, arithmetic and copies ran while one was open for 2% -> 1% of each run, Pallas kernels for 23% -> 17%
where the time goes in v4:
time: 396 us; the launch traced here: 394 us
  blocking collectives  138 us (35%)
  Pallas kernels  102 us (26%)
  waiting for transfers between devices  92.1 us (23%)
  starting transfers between devices  46.4 us (12%)
  local copies, waits for them, and re-layouts  13 us (3%)
    all_to_all x2, blocking collectives, exchange(): return lax.all_to_all(x, 'ctx', split_axis=0, concat_axis=0, tiled=True)  138 us
    all_to_all x5, waiting for transfers between devices, exchange(): return lax.all_to_all(x, 'ctx', split_axis=0, concat_axis=0, tiled=True)  88.9 us
    pallas_call x2, Pallas kernels, transform_chunk(): pl.pallas_call(functools.partial(spectral_kernel, inv_root, scale), out_s...  57.5 us
    all_to_all x5, starting transfers between devices, exchange(): return lax.all_to_all(x, 'ctx', split_axis=0, concat_axis=0, tiled=True)  42.7 us
    pallas_call x1, Pallas kernels, on_device(): pl.pallas_call(functools.partial(exit_kernel, chunks), grid=(steps,), out...  18.8 us
    pallas_call x1, Pallas kernels, on_device(): pl.pallas_call(entry_kernel, grid=(steps,), out_shape=(jax.ShapeDtypeStru...  13.7 us
    pallas_call x1, Pallas kernels, on_device(): pl.pallas_call(unpack_kernel, grid=(steps,), out_shape=whole, in_specs=[p...  9.56 us
  transfers between devices with their start and end apart: 7, of which 7 were waited for; matrix products, arithmetic and copies ran while one was open for 1% of the time, Pallas kernels for 17%

profile of v4, /device:TPU:0, one launch (start us, length us, event | category | flops | bytes accessed | tf_op | source)
XLA Modules:
  0.0 393.9 jit_solution(2383628808537848133)
XLA Ops:
  0.6 0.9 slice.9
  1.5 0.9 slice.10
  2.4 0.9 slice.11
  3.3 2.4 collective-permute-start
  5.7 0.9 collective-permute-done.ahead_ref
  7.2 13.7 %shard_map.163 = (bf16[16,3,256,128]{3,2,1,0:T(8,128)(2,1)}, bf16[16,3,256,128]{3,2,1,0:T(8,128)(2,1)}) custom-call(bf16[256,4096]{1,0:T(8,128)(2,1)} %q_ref.5, bf16[256,4096]{1,0:T(8,128)(2,1)} %k_ref.5, bf16[256,4096]{1,0:T(8,128)(2,1)} %v_ref.5, bf16[256,4096]{1,0:T(8,128)(2,1)} %cot_ref.5, bf16[6,4096]{1,0:T(8,128)(2,1)} %copy-done.5, ...), custom_call_target="tpu_custom_call" | custom-call | flops 100000000 | bytes 12000000 | tf_op jit(solution)/shard_map/pallas_call | solution.py:331
  20.9 79.6 %all_to_all.35.xg_ref = bf16[16,3,256,128]{3,2,1,0:T(8,128)(2,1)} all-to-all(bf16[16,3,256,128]{3,2,1,0:T(8,128)(2,1)} %get-tuple-element.17), channel_id=1, replica_groups=mesh['ctx'=16,'tp'=2] {'ctx'}, dimensions={0} | all-to-all | bytes 6291456 | tf_op jit(solution)/shard_map/all_to_all | solution.py:279
  100.5 5.3 %all-to-all-start.2 = ((bf16[16,3,256,128]{3,2,1,0:T(8,128)(2,1)}), bf16[16,3,256,128]{3,2,1,0:T(8,128)(2,1)S(1)}, u32[]{:S(2)}, u32[]{:S(2)}) async-start(bf16[16,3,256,128]{3,2,1,0:T(8,128)(2,1)} %get-tuple-element.19), calls=%async_computation.2 | async-start | bytes 6291456 | tf_op jit(solution)/shard_map/all_to_all | solution.py:279
  105.8 2.0 broadcast_in_dim.6.cos_ref
  107.9 2.0 broadcast_in_dim.7.sin_ref
  109.9 28.8 %shard_map.164 = (bf16[16,2,256,128]{3,2,1,0:T(8,128)(2,1)}, bf16[16,256,128]{2,1,0:T(8,128)(2,1)}) custom-call(bf16[16,3,256,128]{3,2,1,0:T(8,128)(2,1)} %all_to_all.35.xg_ref, bf16[1024,512]{1,0:T(8,128)(2,1)} %constant.16.clone.first_ref, bf16[512,1024]{1,0:T(8,128)(2,1)} %constant.17.clone.back_ref, bf16[256,256]{1,0:T(8,128)(2,1)} %constant.18.clone.inner_fwd_ref, ...), custom_call_target="tpu_custom_call" | custom-call | flops 12999999488 | bytes 16000000 | tf_op jit(solution)/shard_map/pallas_call | solution.py:160
  138.7 26.5 %all-to-all-done.2.xg_ref = bf16[16,3,256,128]{3,2,1,0:T(8,128)(2,1)S(1)} async-done(((bf16[16,3,256,128]{3,2,1,0:T(8,128)(2,1)}), bf16[16,3,256,128]{3,2,1,0:T(8,128)(2,1)S(1)}, u32[]{:S(2)}, u32[]{:S(2)}) %all-to-all-start.2) | async-done | bytes 3145760 | tf_op jit(solution)/shard_map/all_to_all | solution.py:279
  165.2 1.6 copy-done.2
  166.8 15.4 %all-to-all-start.1 = ((bf16[16,2,256,128]{3,2,1,0:T(8,128)(2,1)}), bf16[16,2,256,128]{3,2,1,0:T(8,128)(2,1)S(1)}, u32[]{:S(2)}, u32[]{:S(2)}) async-start(bf16[16,2,256,128]{3,2,1,0:T(8,128)(2,1)} %get-tuple-element.18), calls=%async_computation.1 | async-start | bytes 4194304 | tf_op jit(solution)/shard_map/all_to_all | solution.py:279
  182.2 28.7 %shard_map.165 = (bf16[16,2,256,128]{3,2,1,0:T(8,128)(2,1)}, bf16[16,256,128]{2,1,0:T(8,128)(2,1)}) custom-call(bf16[16,3,256,128]{3,2,1,0:T(8,128)(2,1)} %copy-done.2, bf16[1024,512]{1,0:T(8,128)(2,1)} %constant.16.clone.first_ref, bf16[512,1024]{1,0:T(8,128)(2,1)} %constant.17.clone.back_ref, bf16[256,256]{1,0:T(8,128)(2,1)} %constant.18.clone.inner_fwd_ref, ...), custom_call_target="tpu_custom_call" | custom-call | flops 12999999488 | bytes 16000000 | tf_op jit(solution)/shard_map/pallas_call | solution.py:160
  211.0 12.4 %all-to-all-done.1.rest_0_ = bf16[16,2,256,128]{3,2,1,0:T(8,128)(2,1)S(1)} async-done(((bf16[16,2,256,128]{3,2,1,0:T(8,128)(2,1)}), bf16[16,2,256,128]{3,2,1,0:T(8,128)(2,1)S(1)}, u32[]{:S(2)}, u32[]{:S(2)}) %all-to-all-start.1) | async-done | bytes 2097184 | tf_op jit(solution)/shard_map/all_to_all | solution.py:279
  223.3 58.6 %all_to_all.36.rest_1_ = bf16[16,2,256,128]{3,2,1,0:T(8,128)(2,1)} all-to-all(bf16[16,2,256,128]{3,2,1,0:T(8,128)(2,1)} %get-tuple-element.20), channel_id=1, replica_groups=mesh['ctx'=16,'tp'=2] {'ctx'}, dimensions={0} | all-to-all | bytes 4194304 | tf_op jit(solution)/shard_map/all_to_all | solution.py:279
  282.0 2.1 shard_map.166
  284.1 1.4 collective-permute-start.1
  285.5 2.3 collective-permute-done.1.behind_ref
  288.5 18.8 %shard_map.167 = (bf16[256,4096]{1,0:T(8,128)(2,1)}, bf16[256,4096]{1,0:T(8,128)(2,1)}, bf16[256,4096]{1,0:T(8,128)(2,1)}, bf16[256,4096]{1,0:T(8,128)(2,1)}, f32[3,3,4096]{2,1,0:T(4,128)}) custom-call(bf16[256,4096]{1,0:T(8,128)(2,1)} %q_ref.5, bf16[256,4096]{1,0:T(8,128)(2,1)} %k_ref.5, bf16[256,4096]{1,0:T(8,128)(2,1)} %v_ref.5, ...), custom_call_target="tpu_custom_call" | custom-call | flops 200000000 | bytes 20000000 | tf_op jit(solution)/shard_map/pallas_call | solution.py:367
  307.3 1.0 reshape_reshape.4
  308.3 0.8 copy.22
  309.1 7.0 %all-to-all-start.4 = ((f32[16,9,256]{2,1,0:T(8,128)}), f32[16,9,256]{2,1,0:T(8,128)S(1)}, u32[]{:S(2)}, u32[]{:S(2)}) async-start(f32[16,9,256]{2,1,0:T(8,128)} %bitcast.6), calls=%async_computation.4 | async-start | bytes 524288 | tf_op jit(solution)/shard_map/all_to_all | solution.py:279
  316.2 1.5 pad_maximum_fusion
  317.7 8.5 %all-to-all-done.4 = f32[16,9,256]{2,1,0:T(8,128)S(1)} async-done(((f32[16,9,256]{2,1,0:T(8,128)}), f32[16,9,256]{2,1,0:T(8,128)S(1)}, u32[]{:S(2)}, u32[]{:S(2)}) %all-to-all-start.4) | async-done | bytes 147488 | tf_op jit(solution)/shard_map/all_to_all | solution.py:279
  326.2 3.7 all-to-all-start.6
  330.0 41.0 %all-to-all-done.6.gf_ref = bf16[16,2,256,128]{3,2,1,0:T(8,128)(2,1)S(1)} async-done(((bf16[16,2,256,128]{3,2,1,0:T(8,128)(2,1)}), bf16[16,2,256,128]{3,2,1,0:T(8,128)(2,1)S(1)}, u32[]{:S(2)}, u32[]{:S(2)}) %all-to-all-start.6) | async-done | bytes 2097184 | tf_op jit(solution)/shard_map/all_to_all | solution.py:279
  371.0 0.8 broadcast_in_dim.8
  371.7 11.2 %all-to-all-start.5 = ((f32[16,9,256]{2,1,0:T(8,128)}), f32[16,9,256]{2,1,0:T(8,128)S(1)}, u32[]{:S(2)}, u32[]{:S(2)}) async-start(f32[16,9,256]{2,1,0:T(8,128)} %broadcast_in_dim.8), calls=%async_computation.5 | async-start | bytes 524288 | tf_op jit(solution)/shard_map/all_to_all | solution.py:279
  382.9 9.6 %shard_map.168 = bf16[256,4096]{1,0:T(8,128)(2,1)} custom-call(bf16[16,2,256,128]{3,2,1,0:T(8,128)(2,1)} %copy-done.1), custom_call_target="tpu_custom_call" | custom-call | tf_op jit(solution)/shard_map/pallas_call | solution.py:380
  393.1 0.8 mul.15
  (22 shorter events, 1.9 us)
Async XLA Ops:
  3.3 3.2 collective-permute-start
  6.5 0.6 copy-start.5
  100.5 5.3 %copy-start.8 = (f32[33,128]{1,0:T(8,128)S(1)}, f32[33,128]{1,0:T(8,128)}, u32[]{:S(2)}) copy-start(f32[33,128]{1,0:T(8,128)} %constant.20.clone) | copy-start | bytes 50692
  100.5 64.7 %all-to-all-start.2 = ((bf16[16,3,256,128]{3,2,1,0:T(8,128)(2,1)}), bf16[16,3,256,128]{3,2,1,0:T(8,128)(2,1)S(1)}, u32[]{:S(2)}, u32[]{:S(2)}) async-start(bf16[16,3,256,128]{3,2,1,0:T(8,128)(2,1)} %get-tuple-element.19), calls=%async_computation.2 | async-start | bytes 6291456 | tf_op jit(solution)/shard_map/all_to_all | solution.py:279
  105.8 2.1 copy-start.7
  165.2 1.6 copy-start.2
  166.8 56.5 %all-to-all-start.1 = ((bf16[16,2,256,128]{3,2,1,0:T(8,128)(2,1)}), bf16[16,2,256,128]{3,2,1,0:T(8,128)(2,1)S(1)}, u32[]{:S(2)}, u32[]{:S(2)}) async-start(bf16[16,2,256,128]{3,2,1,0:T(8,128)(2,1)} %get-tuple-element.18), calls=%async_computation.1 | async-start | bytes 4194304 | tf_op jit(solution)/shard_map/all_to_all | solution.py:279
  223.3 58.6 %copy-start = (bf16[16,2,256,128]{3,2,1,0:T(8,128)(2,1)}, bf16[16,2,256,128]{3,2,1,0:T(8,128)(2,1)S(1)}, u32[]{:S(2)}) copy-start(bf16[16,2,256,128]{3,2,1,0:T(8,128)(2,1)S(1)} %all-to-all-done.1.rest_0_) | copy-start | bytes 6291460
  284.1 32.0 %copy-start.3 = (bf16[16,256,128]{2,1,0:T(8,128)(2,1)S(1)}, bf16[16,256,128]{2,1,0:T(8,128)(2,1)}, u32[]{:S(2)}) copy-start(bf16[16,256,128]{2,1,0:T(8,128)(2,1)} %get-tuple-element.26) | copy-start | bytes 3145732
  284.1 32.1 %copy-start.4 = (bf16[16,256,128]{2,1,0:T(8,128)(2,1)S(1)}, bf16[16,256,128]{2,1,0:T(8,128)(2,1)}, u32[]{:S(2)}) copy-start(bf16[16,256,128]{2,1,0:T(8,128)(2,1)} %get-tuple-element.27) | copy-start | bytes 3145732
  284.1 3.7 collective-permute-start.1
  287.9 0.6 copy-start.6
  309.1 17.1 %all-to-all-start.4 = ((f32[16,9,256]{2,1,0:T(8,128)}), f32[16,9,256]{2,1,0:T(8,128)S(1)}, u32[]{:S(2)}, u32[]{:S(2)}) async-start(f32[16,9,256]{2,1,0:T(8,128)} %bitcast.6), calls=%async_computation.4 | async-start | bytes 524288 | tf_op jit(solution)/shard_map/all_to_all | solution.py:279
  326.2 44.8 %all-to-all-start.6 = ((bf16[16,2,256,128]{3,2,1,0:T(8,128)(2,1)}), bf16[16,2,256,128]{3,2,1,0:T(8,128)(2,1)S(1)}, u32[]{:S(2)}, u32[]{:S(2)}) async-start(bf16[16,2,256,128]{3,2,1,0:T(8,128)(2,1)} %pad_maximum_fusion), calls=%async_computation.6 | async-start | bytes 4194304 | tf_op jit(solution)/shard_map/all_to_all | solution.py:279
  371.0 12.0 %copy-start.1 = (bf16[16,2,256,128]{3,2,1,0:T(8,128)(2,1)}, bf16[16,2,256,128]{3,2,1,0:T(8,128)(2,1)S(1)}, u32[]{:S(2)}) copy-start(bf16[16,2,256,128]{3,2,1,0:T(8,128)(2,1)S(1)} %all-to-all-done.6.gf_ref) | copy-start | bytes 6291460
  371.7 21.2 %all-to-all-start.5 = ((f32[16,9,256]{2,1,0:T(8,128)}), f32[16,9,256]{2,1,0:T(8,128)S(1)}, u32[]{:S(2)}, u32[]{:S(2)}) async-start(f32[16,9,256]{2,1,0:T(8,128)} %broadcast_in_dim.8), calls=%async_computation.5 | async-start | bytes 524288 | tf_op jit(solution)/shard_map/all_to_all | solution.py:279
